TPU v7x, 32 devices: a whole 2x2x4 slice. The times are simulated.
32 devices in a mesh: sector: 16 (over z, x, core), harm: 2 (over y).
Axes of the slice: x: 2, y: 2, z: 4, core: 2. Of those that a mesh axis runs over, the one named last changes fastest.
Arguments:
- disp: float32 [16, 3, 64, 1024], P('sector', None, 'harm'), may hold values from -0.6 to 0.6
- direction: float32 [16, 3, 64, 1024], P('sector', None, 'harm'), may hold values from -0.6 to 0.6
- stick_state: int32 [16, 128, 1024], P('sector'), may hold values from 0 to 2
- contact_params: float32 [16, 4, 1024], P('sector'), may hold values from 0.3 to 3
- mistuning: float32 [16], replicated, may hold values from 1 to 4
- group_ids: int32 [16], replicated, may hold values from 0 to 3, never falling along the last dimension, each value on 1 to 8 neighbouring positions
- diag_stiff: float32 [64, 16], P('harm'), may hold values from 1 to 10
- cross_stiff: float32 [64, 16], P('harm'), may hold values from -3 to 3
- excitation: float32 [3, 64, 1024, 16], P(None, 'harm', 'sector'), may hold values from -1.8 to 1.8
Outputs:
- residual: float32 [3, 64, 1024, 16], P(None, 'harm', 'sector')
- jvp: float32 [3, 64, 1024, 16], P(None, 'harm', 'sector')
Inputs may be any that keep to these rules, and one draw needn't show every extreme that they name: `group_ids`: the sectors of one group are consecutive and ids never fall; each of the 4 groups holds 1 to 8 sectors.
All inputs are finite; a program needn't handle non-finite values.
Results may differ from a plain program's by a relative error of at most 0.0003.
Values sent between devices are 32-bit elements; how exact they have to be, the bound alone decides.
A program may use at most 64 MiB of HBM per device.

v0:
```python
import math

import jax
import jax.numpy as jnp
from jax import lax
from jax.sharding import PartitionSpec as P

exact_mode = lax.Precision.HIGHEST


def passed_along(value, axis, steps):
    count = lax.axis_size(axis)
    pairs = [(source, (source + steps) % count) for source in range(count)]
    return lax.ppermute(value, axis, pairs)


def from_behind(block, axis, distance):
    devices = range(lax.axis_size(axis))
    route = [(i - distance, i) for i in devices if i - distance in devices]
    return lax.ppermute(block, axis, route)


def basis_table(coefs, samples):
    coef_index = lax.broadcasted_iota(jnp.int32, (coefs, samples), 0)
    time_index = lax.broadcasted_iota(jnp.int32, (coefs, samples), 1)
    harmonic = coef_index // 2 + 1
    phase = harmonic * time_index % samples
    angle = phase.astype(jnp.float32) * (2.0 * math.pi / samples)
    return jnp.where(coef_index % 2 == 0, jnp.cos(angle), jnp.sin(angle))


def hartley_table(count):
    row_index = lax.broadcasted_iota(jnp.int32, (count, count), 0)
    col_index = lax.broadcasted_iota(jnp.int32, (count, count), 1)
    phase = row_index * col_index % count
    angle = phase.astype(jnp.float32) * (2.0 * math.pi / count)
    return (jnp.cos(angle) + jnp.sin(angle)) / math.sqrt(count)


def contact_law(gaps, dgaps, states_here, params):
    preload = params[0]
    normal_stiff = params[1]
    tangent_stiff = params[2]
    friction_coef = params[3]
    touching = (states_here != 2).astype(jnp.float32)
    sliding = states_here == 1
    normal = (preload + normal_stiff * gaps[0]) * touching
    dnormal = normal_stiff * dgaps[0] * touching
    radius = jnp.sqrt(gaps[1] * gaps[1] + gaps[2] * gaps[2] + 1.0)
    projected = (gaps[1] * dgaps[1] + gaps[2] * dgaps[2]) / (radius * radius * radius)
    tractions = [normal]
    dtractions = [dnormal]
    for channel in (1, 2):
        stuck = tangent_stiff * gaps[channel]
        dstuck = tangent_stiff * dgaps[channel]
        slipped = friction_coef * normal * gaps[channel] / radius
        dslipped = friction_coef * (
            dnormal * gaps[channel] / radius
            + normal * (dgaps[channel] / radius - gaps[channel] * projected)
        )
        tractions.append(jnp.where(sliding, slipped, stuck) * touching)
        dtractions.append(jnp.where(sliding, dslipped, dstuck) * touching)
    return (jnp.stack(tractions), jnp.stack(dtractions))


def mirror(field):
    return jnp.roll(jnp.flip(field, -1), 1, -1)


def group_flag(group_ids, own_group, other_index, sectors):
    inside = jnp.logical_and(other_index >= 0, other_index < sectors)
    safe_index = jnp.clip(other_index, 0, sectors - 1)
    other_group = lax.dynamic_slice_in_dim(group_ids, safe_index, 1)
    return jnp.logical_and(inside, other_group == own_group).astype(jnp.float32)[0]


def body(
    disp,
    direction,
    stick_state,
    contact_params,
    mistuning,
    group_ids,
    diag_stiff,
    cross_stiff,
    excitation,
):
    sectors = lax.axis_size("sector")
    sector_index = lax.axis_index("sector")
    harm_index = lax.axis_index("harm")
    local_coefs = disp.shape[2]
    samples = stick_state.shape[1]
    coefs = local_coefs * lax.axis_size("harm")
    table = basis_table(coefs, samples)
    own_table = lax.dynamic_slice_in_dim(table, harm_index * local_coefs, local_coefs, 0)
    scale = 2.0 / samples
    hartley = hartley_table(sectors)
    paired = jnp.concatenate([disp, direction], 0)
    paired_next = passed_along(paired, "sector", -1)
    relative = paired - paired_next
    gathered = lax.all_gather(relative, "harm", axis=2, tiled=True)
    params_here = contact_params[0]
    gaps = jnp.einsum("wcjp,jt->wctp", gathered, table, precision=exact_mode)
    traction, dtraction = contact_law(gaps[0], gaps[1], stick_state[0], params_here)
    loads = (
        jnp.einsum(
            "wctp,jt->wcjp", jnp.stack([traction, dtraction]), own_table, precision=exact_mode
        )
        * scale
    )
    earlier_loads = passed_along(loads, "sector", 1)
    own_group = lax.dynamic_slice_in_dim(group_ids, sector_index, 1)
    members = jnp.sum((group_ids == own_group[0]).astype(jnp.float32))
    totals = paired
    for offset in range(1, 8):
        from_before = from_behind(paired, "sector", offset)
        from_after = from_behind(paired, "sector", -offset)
        flag_before = group_flag(group_ids, own_group, sector_index - offset, sectors)
        flag_after = group_flag(group_ids, own_group, sector_index + offset, sectors)
        totals = totals + flag_before * from_before + flag_after * from_after
    weight = lax.dynamic_slice_in_dim(mistuning, sector_index, 1)[0]
    forces = loads - earlier_loads + weight * (paired - totals / members)
    outgoing = jnp.concatenate([paired, forces], 0)
    received = lax.all_to_all(outgoing[:, None], "sector", split_axis=4, concat_axis=1, tiled=True)
    states_nd = jnp.einsum("ks,wscjp->wcjpk", hartley, received[0:2], precision=exact_mode)
    forces_nd = jnp.einsum("ks,wscjp->wcjpk", hartley, received[2:4], precision=exact_mode)
    stiff_diag = diag_stiff[None, :, None, :]
    stiff_cross = cross_stiff[None, :, None, :]
    residual = (
        stiff_diag * states_nd[0] + stiff_cross * mirror(states_nd[0]) + forces_nd[0] - excitation
    )
    jvp = stiff_diag * states_nd[1] + stiff_cross * mirror(states_nd[1]) + forces_nd[1]
    return (residual, jvp)


def solution(mesh):
    in_specs = (
        P("sector", None, "harm", None),
        P("sector", None, "harm", None),
        P("sector", None, None),
        P("sector", None, None),
        P(),
        P(),
        P("harm", None),
        P("harm", None),
        P(None, "harm", "sector", None),
    )
    out_specs = (P(None, "harm", "sector", None), P(None, "harm", "sector", None))
    return jax.shard_map(body, mesh=mesh, in_specs=in_specs, out_specs=out_specs, check_vma=False)
```

profile of v0, /device:TPU:0, one launch (start us, length us, event | category | flops | bytes accessed | tf_op | source)
XLA Modules:
  0.0 285.8 jit_solution(17218684474159676690)
XLA Ops:
  7.2 1.0 constant_dynamic-update-slice_fusion.1
  8.2 1.0 constant_dynamic-update-slice_fusion
  9.3 5.5 %collective-permute-start = (f32[2,3,32,1024]{3,2,1,0:T(8,128)S(1)}, f32[2,3,32,1024]{3,2,1,0:T(8,128)S(1)}, u32[]{:S(2)}, u32[]{:S(2)}) collective-permute-start(f32[2,3,32,1024]{3,2,1,0:T(8,128)S(1)} %constant_dynamic-update-slice_fusion), channel_id=1, source_target_pairs={{0,30},{2,0},{4,2},{6,4},{8,6},{10,8},{12,10},{14,12},{16,14},{18,... | collective-permute-start | bytes 2359304 | tf_op jit(solution)/shard_map/ppermute | solution.py:14
  14.7 9.5 %collective-permute-done = f32[2,3,32,1024]{3,2,1,0:T(8,128)S(1)} collective-permute-done((f32[2,3,32,1024]{3,2,1,0:T(8,128)S(1)}, f32[2,3,32,1024]{3,2,1,0:T(8,128)S(1)}, u32[]{:S(2)}, u32[]{:S(2)}) %collective-permute-start) | collective-permute-done | bytes 786464 | tf_op jit(solution)/shard_map/ppermute | solution.py:14
  24.3 1.0 sub.66
  25.2 1.3 collective-permute-start.10
  26.6 1.3 collective-permute-start.11
  27.9 5.5 %collective-permute-start.12 = (f32[2,3,32,1024]{3,2,1,0:T(8,128)S(1)}, f32[2,3,32,1024]{3,2,1,0:T(8,128)S(1)}, u32[]{:S(2)}, u32[]{:S(2)}) collective-permute-start(f32[2,3,32,1024]{3,2,1,0:T(8,128)S(1)} %constant_dynamic-update-slice_fusion), channel_id=1, source_target_pairs={{0,12},{2,14},{4,16},{6,18},{8,20},{10,22},{12,24},{14,26},{16,28}... | collective-permute-start | bytes 2359304 | tf_op jit(solution)/shard_map/ppermute | solution.py:20
  33.4 1.3 collective-permute-start.13
  34.7 6.0 %collective-permute-start.14 = (f32[2,3,32,1024]{3,2,1,0:T(8,128)S(1)}, f32[2,3,32,1024]{3,2,1,0:T(8,128)}, u32[]{:S(2)}, u32[]{:S(2)}) collective-permute-start(f32[2,3,32,1024]{3,2,1,0:T(8,128)S(1)} %constant_dynamic-update-slice_fusion), channel_id=1, source_target_pairs={{0,14},{2,16},{4,18},{6,20},{8,22},{10,24},{12,26},{14,28},{16,30}... | collective-permute-start | bytes 2359304 | tf_op jit(solution)/shard_map/ppermute | solution.py:20
  41.0 13.0 %all-gather.2.cloned.1.call-done = f32[2,3,64,1024]{3,2,1,0:T(8,128)} async-done(((f32[2,3,32,1024]{3,2,1,0:T(8,128)}), f32[2,3,64,1024]{3,2,1,0:T(8,128)}) %all-gather.2.cloned.1.call-update) | async-done | bytes 1572880 | tf_op jit(solution)/shard_map/all_gather | solution.py:101
  54.0 4.4 %convolution_bitcast_fusion = f32[2,3,128,1024]{3,2,1,0:T(8,128)S(1)} fusion(f32[2,3,64,1024]{3,2,1,0:T(8,128)} %all-gather.2.cloned.1.call-done, s32[64]{0:T(128)S(1)} %get-tuple-element.34, s32[64]{0:T(128)S(1)} %get-tuple-element.36, s32[64]{0:T(128)S(1)} %get-tuple-element.35, s32[64]{0:T(128)S(1)} %get-tuple-element.37, ...), kind=kOutput, calls=%fused_computation.4 | convolution fusion | flops 604135424 | bytes 4719744 | tf_op jit(solution)/shard_map/wcjp,jt->wctp/dot_general | solution.py:103
  58.8 0.7 select_select_fusion.1
  59.5 1.3 collective-permute-start.15
  60.8 1.8 collective-permute-start.2
  62.6 14.2 %collective-permute-done.12 = f32[2,3,32,1024]{3,2,1,0:T(8,128)S(1)} collective-permute-done((f32[2,3,32,1024]{3,2,1,0:T(8,128)S(1)}, f32[2,3,32,1024]{3,2,1,0:T(8,128)S(1)}, u32[]{:S(2)}, u32[]{:S(2)}) %collective-permute-start.12) | collective-permute-done | bytes 786464 | tf_op jit(solution)/shard_map/ppermute | solution.py:20
  76.8 1.3 collective-permute-start.3
  78.1 35.0 %collective-permute-start.4 = (f32[2,3,32,1024]{3,2,1,0:T(8,128)S(1)}, f32[2,3,32,1024]{3,2,1,0:T(8,128)S(1)}, u32[]{:S(2)}, u32[]{:S(2)}) collective-permute-start(f32[2,3,32,1024]{3,2,1,0:T(8,128)S(1)} %constant_dynamic-update-slice_fusion), channel_id=1, source_target_pairs={{0,4},{2,6},{4,8},{6,10},{8,12},{10,14},{12,16},{14,18},{16,20},{1... | collective-permute-start | bytes 2359304 | tf_op jit(solution)/shard_map/ppermute | solution.py:20
  113.0 1.3 collective-permute-start.5
  114.5 0.6 select_select_fusion
  115.3 1.7 fusion.9
  117.0 2.2 collective-permute-start.6
  119.2 1.3 collective-permute-start.7
  120.5 13.2 %collective-permute-start.8 = (f32[2,3,32,1024]{3,2,1,0:T(8,128)S(1)}, f32[2,3,32,1024]{3,2,1,0:T(8,128)}, u32[]{:S(2)}, u32[]{:S(2)}) collective-permute-start(f32[2,3,32,1024]{3,2,1,0:T(8,128)S(1)} %constant_dynamic-update-slice_fusion), channel_id=1, source_target_pairs={{0,8},{2,10},{4,12},{6,14},{8,16},{10,18},{12,20},{14,22},{16,24},... | collective-permute-start | bytes 2359304 | tf_op jit(solution)/shard_map/ppermute | solution.py:20
  133.7 24.6 %collective-permute-done.4 = f32[2,3,32,1024]{3,2,1,0:T(8,128)S(1)} collective-permute-done((f32[2,3,32,1024]{3,2,1,0:T(8,128)S(1)}, f32[2,3,32,1024]{3,2,1,0:T(8,128)S(1)}, u32[]{:S(2)}, u32[]{:S(2)}) %collective-permute-start.4) | collective-permute-done | bytes 786464 | tf_op jit(solution)/shard_map/ppermute | solution.py:20
  158.2 1.3 collective-permute-start.9
  159.6 0.9 copy-done.8
  160.5 0.7 fusion.59
  179.8 0.7 dynamic_slice.52
  180.5 1.4 fusion.38
  181.9 5.4 %collective-permute-done.1 = f32[2,3,32,1024]{3,2,1,0:T(8,128)} collective-permute-done((f32[2,3,32,1024]{3,2,1,0:T(8,128)S(1)}, f32[2,3,32,1024]{3,2,1,0:T(8,128)}, u32[]{:S(2)}, u32[]{:S(2)}) %collective-permute-start.1) | collective-permute-done | bytes 786464 | tf_op jit(solution)/shard_map/ppermute | solution.py:14
  187.3 7.0 %multiply_add_fusion = f32[2,3,32,1024]{3,2,1,0:T(8,128)S(1)} fusion(f32[2,3,32,1024]{3,2,1,0:T(8,128)S(1)} %constant_dynamic-update-slice_fusion, f32[2,3,32,1024]{3,2,1,0:T(8,128)} %copy-done.4, f32[2,3,32,1024]{3,2,1,0:T(8,128)} %collective-permute-done.14, f32[2,3,32,1024]{3,2,1,0:T(8,128)} %collective-permute-done.13, f32[2,3,32,1024]{3,2,1,0:T(8,128)} %copy-done.3, ...), kind=kLoop, calls=%fused_computation.25 | loop fusion | flops 6488064 | bytes 14155840 | tf_op jit(solution)/shard_map/add | solution.py:122
  194.5 4.6 %copy.18 = f32[4,1,3,32,1024]{3,0,2,1,4:T(4,128)} copy(f32[4,1,3,32,1024]{4,3,2,0,1:T(8,128)S(1)} %maximum_bitcast_fusion.2) | data formatting | bytes 3145728 | tf_op jit(solution)/shard_map/broadcast_in_dim | solution.py:124
  199.1 7.0 %reshape.518 = f32[16,1,24576]{2,1,0:T(1,128)} reshape(f32[1024,1,3,4,32]{4,3,2,1,0:T(4,128)} %bitcast.139) | data formatting | bytes 3145728
  206.1 9.9 %all-to-all-start = ((f32[16,1,24576]{2,1,0:T(1,128)}), f32[16,1,24576]{2,1,0:T(1,128)S(1)}, u32[]{:S(2)}, u32[]{:S(2)}) async-start(f32[16,1,24576]{2,1,0:T(1,128)} %reshape.518), calls=%async_computation | async-start | bytes 3145728 | tf_op jit(solution)/shard_map/all_to_all | solution.py:124
  216.1 31.8 %all-to-all-done = f32[16,1,24576]{2,1,0:T(1,128)S(1)} async-done(((f32[16,1,24576]{2,1,0:T(1,128)}), f32[16,1,24576]{2,1,0:T(1,128)S(1)}, u32[]{:S(2)}, u32[]{:S(2)}) %all-to-all-start) | async-done | bytes 1572896 | tf_op jit(solution)/shard_map/all_to_all | solution.py:124
  247.9 0.5 broadcast.307
  248.4 4.4 %reduce = f32[16,24576]{1,0:T(8,128)S(1)} reduce(f32[16,1,24576]{2,1,0:T(1,128)S(1)} %all-to-all-done, f32[]{:T(128)} %broadcast.307), dimensions={1}, to_apply=%all_to_all.11.reduce_sub_computation | reduce | bytes 3145732 | tf_op jit(solution)/shard_map/all_to_all | solution.py:124
  252.9 4.9 %reshape.519 = f32[1024,1,3,4,32]{4,3,2,1,0:T(4,128)} reshape(f32[16,24576]{1,0:T(8,128)S(1)} %reduce) | data formatting | bytes 3145728
  257.8 6.8 %copy.24 = f32[4,1,3,32,16,64]{5,4,3,2,0,1:T(8,128)} copy(f32[4,1,3,32,16,64]{3,0,2,5,4,1:T(4,128)} %bitcast.138) | data formatting | bytes 3145728 | tf_op jit(solution)/shard_map/all_to_all | solution.py:124
  264.6 2.9 %fusion.5 = f32[2,3,32,64,16]{3,4,2,1,0:T(8,128)S(1)} fusion(f32[4,16,1,3,32,64]{5,1,4,3,0,2:T(8,128)} %bitcast.140), kind=kOutput, calls=%fused_computation.8 | convolution fusion | flops 37752832 | bytes 2359296 | tf_op jit(solution)/shard_map/ks,wscjp->wcjpk/dot_general | solution.py:125
  267.6 0.9 slice.145
  268.6 0.9 slice.150
  269.6 0.5 copy-done
  270.1 1.5 fusion.4
  271.6 2.1 slice.127
  273.6 2.0 slice.134
  275.7 3.3 %fusion.12 = (f32[3,32,64,16]{2,3,1,0:T(8,128)}, f32[3,32,64,16]{2,3,1,0:T(8,128)}) fusion(f32[2,3,32,64,16]{3,4,2,1,0:T(8,128)S(1)} %fusion.4, f32[3,32,64,15]{2,3,1,0:T(8,128)} %slice.134, f32[3,32,64,1]{2,3,1,0:T(1,128)S(1)} %slice.149, f32[32,16]{1,0:T(8,128)S(1)} %copy.20, f32[32,16]{1,0:T(8,128)S(1)} %copy.17, f32[2,3,32,64,16]{3,4,2,1,0:T(8,128)S(1)} %fusion.5, ...), kind=kLoop, calls=%fused_computation.15 | loop fusion | flops 1081344 | bytes 3543040 | tf_op jit(solution)/shard_map/add | solution.py:132
  (57 shorter events, 1.5 us)
Async XLA Ops:
  7.2 46.8 %all-gather.2.cloned.1.call-start = ((), (), s32[]{:S(2)}) async-start(), calls=%async_computation.1 | async-start | bytes 2359296 | tf_op jit(solution)/shard_map/all_gather | solution.py:101
  9.3 31.4 %copy-start.11 = (f32[1,4,1024]{2,1,0:T(4,128)S(1)}, f32[1,4,1024]{2,1,0:T(4,128)}, u32[]{:S(2)}) copy-start(f32[1,4,1024]{2,1,0:T(4,128)} %param.12) | copy-start | bytes 49156
  9.3 15.0 %collective-permute-start = (f32[2,3,32,1024]{3,2,1,0:T(8,128)S(1)}, f32[2,3,32,1024]{3,2,1,0:T(8,128)S(1)}, u32[]{:S(2)}, u32[]{:S(2)}) collective-permute-start(f32[2,3,32,1024]{3,2,1,0:T(8,128)S(1)} %constant_dynamic-update-slice_fusion), channel_id=1, source_target_pairs={{0,30},{2,0},{4,2},{6,4},{8,6},{10,8},{12,10},{14,12},{16,14},{18,... | collective-permute-start | bytes 2359304 | tf_op jit(solution)/shard_map/ppermute | solution.py:14
  25.2 34.3 %collective-permute-start.10 = (f32[2,3,32,1024]{3,2,1,0:T(8,128)S(1)}, f32[2,3,32,1024]{3,2,1,0:T(8,128)S(1)}, u32[]{:S(2)}, u32[]{:S(2)}) collective-permute-start(f32[2,3,32,1024]{3,2,1,0:T(8,128)S(1)} %constant_dynamic-update-slice_fusion), channel_id=1, source_target_pairs={{0,10},{2,12},{4,14},{6,16},{8,18},{10,20},{12,22},{14,24},{16,26}... | collective-permute-start | bytes 2359304 | tf_op jit(solution)/shard_map/ppermute | solution.py:20
  26.6 34.2 %collective-permute-start.11 = (f32[2,3,32,1024]{3,2,1,0:T(8,128)S(1)}, f32[2,3,32,1024]{3,2,1,0:T(8,128)S(1)}, u32[]{:S(2)}, u32[]{:S(2)}) collective-permute-start(f32[2,3,32,1024]{3,2,1,0:T(8,128)S(1)} %constant_dynamic-update-slice_fusion), channel_id=1, source_target_pairs={{10,0},{12,2},{14,4},{16,6},{18,8},{20,10},{22,12},{24,14},{26,16}... | collective-permute-start | bytes 2359304 | tf_op jit(solution)/shard_map/ppermute | solution.py:20
  27.9 48.9 %collective-permute-start.12 = (f32[2,3,32,1024]{3,2,1,0:T(8,128)S(1)}, f32[2,3,32,1024]{3,2,1,0:T(8,128)S(1)}, u32[]{:S(2)}, u32[]{:S(2)}) collective-permute-start(f32[2,3,32,1024]{3,2,1,0:T(8,128)S(1)} %constant_dynamic-update-slice_fusion), channel_id=1, source_target_pairs={{0,12},{2,14},{4,16},{6,18},{8,20},{10,22},{12,24},{14,26},{16,28}... | collective-permute-start | bytes 2359304 | tf_op jit(solution)/shard_map/ppermute | solution.py:20
  33.4 44.7 %collective-permute-start.13 = (f32[2,3,32,1024]{3,2,1,0:T(8,128)S(1)}, f32[2,3,32,1024]{3,2,1,0:T(8,128)}, u32[]{:S(2)}, u32[]{:S(2)}) collective-permute-start(f32[2,3,32,1024]{3,2,1,0:T(8,128)S(1)} %constant_dynamic-update-slice_fusion), channel_id=1, source_target_pairs={{12,0},{14,2},{16,4},{18,6},{20,8},{22,10},{24,12},{26,14},{28,16}... | collective-permute-start | bytes 2359304 | tf_op jit(solution)/shard_map/ppermute | solution.py:20
  34.7 78.3 %collective-permute-start.14 = (f32[2,3,32,1024]{3,2,1,0:T(8,128)S(1)}, f32[2,3,32,1024]{3,2,1,0:T(8,128)}, u32[]{:S(2)}, u32[]{:S(2)}) collective-permute-start(f32[2,3,32,1024]{3,2,1,0:T(8,128)S(1)} %constant_dynamic-update-slice_fusion), channel_id=1, source_target_pairs={{0,14},{2,16},{4,18},{6,20},{8,22},{10,24},{12,26},{14,28},{16,30}... | collective-permute-start | bytes 2359304 | tf_op jit(solution)/shard_map/ppermute | solution.py:20
  54.0 4.4 %copy-start.9 = (s32[1,128,1024]{2,1,0:T(8,128)S(1)}, s32[1,128,1024]{2,1,0:T(8,128)}, u32[]{:S(2)}) copy-start(s32[1,128,1024]{2,1,0:T(8,128)} %param.11) | copy-start | bytes 1572868
  59.5 57.5 %collective-permute-start.15 = (f32[2,3,32,1024]{3,2,1,0:T(8,128)S(1)}, f32[2,3,32,1024]{3,2,1,0:T(8,128)S(1)}, u32[]{:S(2)}, u32[]{:S(2)}) collective-permute-start(f32[2,3,32,1024]{3,2,1,0:T(8,128)S(1)} %constant_dynamic-update-slice_fusion), channel_id=1, source_target_pairs={{14,0},{16,2},{18,4},{20,6},{22,8},{24,10},{26,12},{28,14},{30,16}... | collective-permute-start | bytes 2359304 | tf_op jit(solution)/shard_map/ppermute | solution.py:20
  60.8 58.4 %collective-permute-start.2 = (f32[2,3,32,1024]{3,2,1,0:T(8,128)S(1)}, f32[2,3,32,1024]{3,2,1,0:T(8,128)S(1)}, u32[]{:S(2)}, u32[]{:S(2)}) collective-permute-start(f32[2,3,32,1024]{3,2,1,0:T(8,128)S(1)} %constant_dynamic-update-slice_fusion), channel_id=1, source_target_pairs={{0,2},{2,4},{4,6},{6,8},{8,10},{10,12},{12,14},{14,16},{16,18},{18... | collective-permute-start | bytes 2359304 | tf_op jit(solution)/shard_map/ppermute | solution.py:20
  76.8 37.7 %copy-start.3 = (f32[2,3,32,1024]{3,2,1,0:T(8,128)}, f32[2,3,32,1024]{3,2,1,0:T(8,128)S(1)}, u32[]{:S(2)}) copy-start(f32[2,3,32,1024]{3,2,1,0:T(8,128)S(1)} %collective-permute-done.12) | copy-start | bytes 2359300
  76.8 43.7 %collective-permute-start.3 = (f32[2,3,32,1024]{3,2,1,0:T(8,128)S(1)}, f32[2,3,32,1024]{3,2,1,0:T(8,128)S(1)}, u32[]{:S(2)}, u32[]{:S(2)}) collective-permute-start(f32[2,3,32,1024]{3,2,1,0:T(8,128)S(1)} %constant_dynamic-update-slice_fusion), channel_id=1, source_target_pairs={{2,0},{4,2},{6,4},{8,6},{10,8},{12,10},{14,12},{16,14},{18,16},{20... | collective-permute-start | bytes 2359304 | tf_op jit(solution)/shard_map/ppermute | solution.py:20
  78.1 80.1 %collective-permute-start.4 = (f32[2,3,32,1024]{3,2,1,0:T(8,128)S(1)}, f32[2,3,32,1024]{3,2,1,0:T(8,128)S(1)}, u32[]{:S(2)}, u32[]{:S(2)}) collective-permute-start(f32[2,3,32,1024]{3,2,1,0:T(8,128)S(1)} %constant_dynamic-update-slice_fusion), channel_id=1, source_target_pairs={{0,4},{2,6},{4,8},{6,10},{8,12},{10,14},{12,16},{14,18},{16,20},{1... | collective-permute-start | bytes 2359304 | tf_op jit(solution)/shard_map/ppermute | solution.py:20
  113.0 46.5 %collective-permute-start.5 = (f32[2,3,32,1024]{3,2,1,0:T(8,128)S(1)}, f32[2,3,32,1024]{3,2,1,0:T(8,128)S(1)}, u32[]{:S(2)}, u32[]{:S(2)}) collective-permute-start(f32[2,3,32,1024]{3,2,1,0:T(8,128)S(1)} %constant_dynamic-update-slice_fusion), channel_id=1, source_target_pairs={{4,0},{6,2},{8,4},{10,6},{12,8},{14,10},{16,12},{18,14},{20,16},{2... | collective-permute-start | bytes 2359304 | tf_op jit(solution)/shard_map/ppermute | solution.py:20
  115.2 45.2 %copy-start.10 = (s32[16]{0:T(128)S(1)}, s32[16]{0:T(128)}, u32[]{:S(2)}) copy-start(s32[16]{0:T(128)} %param.14) | copy-start | bytes 196
  115.3 64.5 %copy-start.14 = (f32[16]{0:T(128)S(1)}, f32[16]{0:T(128)}, u32[]{:S(2)}) copy-start(f32[16]{0:T(128)} %param.13) | copy-start | bytes 196
  117.0 42.5 %copy-start.4 = (f32[2,3,32,1024]{3,2,1,0:T(8,128)}, f32[2,3,32,1024]{3,2,1,0:T(8,128)S(1)}, u32[]{:S(2)}) copy-start(f32[2,3,32,1024]{3,2,1,0:T(8,128)S(1)} %collective-permute-done.15) | copy-start | bytes 2359300
  117.0 64.8 %collective-permute-start.6 = (f32[2,3,32,1024]{3,2,1,0:T(8,128)S(1)}, f32[2,3,32,1024]{3,2,1,0:T(8,128)}, u32[]{:S(2)}, u32[]{:S(2)}) collective-permute-start(f32[2,3,32,1024]{3,2,1,0:T(8,128)S(1)} %constant_dynamic-update-slice_fusion), channel_id=1, source_target_pairs={{0,6},{2,8},{4,10},{6,12},{8,14},{10,16},{12,18},{14,20},{16,22},{... | collective-permute-start | bytes 2359304 | tf_op jit(solution)/shard_map/ppermute | solution.py:20
  119.2 40.4 %copy-start.5 = (f32[2,3,32,1024]{3,2,1,0:T(8,128)}, f32[2,3,32,1024]{3,2,1,0:T(8,128)S(1)}, u32[]{:S(2)}) copy-start(f32[2,3,32,1024]{3,2,1,0:T(8,128)S(1)} %collective-permute-done.2) | copy-start | bytes 2359300
  119.2 62.7 %collective-permute-start.7 = (f32[2,3,32,1024]{3,2,1,0:T(8,128)S(1)}, f32[2,3,32,1024]{3,2,1,0:T(8,128)}, u32[]{:S(2)}, u32[]{:S(2)}) collective-permute-start(f32[2,3,32,1024]{3,2,1,0:T(8,128)S(1)} %constant_dynamic-update-slice_fusion), channel_id=1, source_target_pairs={{6,0},{8,2},{10,4},{12,6},{14,8},{16,10},{18,12},{20,14},{22,16},{... | collective-permute-start | bytes 2359304 | tf_op jit(solution)/shard_map/ppermute | solution.py:20
  120.5 39.1 %copy-start.6 = (f32[2,3,32,1024]{3,2,1,0:T(8,128)}, f32[2,3,32,1024]{3,2,1,0:T(8,128)S(1)}, u32[]{:S(2)}) copy-start(f32[2,3,32,1024]{3,2,1,0:T(8,128)S(1)} %collective-permute-done.3) | copy-start | bytes 2359300
  120.5 61.3 %collective-permute-start.8 = (f32[2,3,32,1024]{3,2,1,0:T(8,128)S(1)}, f32[2,3,32,1024]{3,2,1,0:T(8,128)}, u32[]{:S(2)}, u32[]{:S(2)}) collective-permute-start(f32[2,3,32,1024]{3,2,1,0:T(8,128)S(1)} %constant_dynamic-update-slice_fusion), channel_id=1, source_target_pairs={{0,8},{2,10},{4,12},{6,14},{8,16},{10,18},{12,20},{14,22},{16,24},... | collective-permute-start | bytes 2359304 | tf_op jit(solution)/shard_map/ppermute | solution.py:20
  158.2 1.3 copy-start.7
  158.2 23.6 %collective-permute-start.9 = (f32[2,3,32,1024]{3,2,1,0:T(8,128)S(1)}, f32[2,3,32,1024]{3,2,1,0:T(8,128)}, u32[]{:S(2)}, u32[]{:S(2)}) collective-permute-start(f32[2,3,32,1024]{3,2,1,0:T(8,128)S(1)} %constant_dynamic-update-slice_fusion), channel_id=1, source_target_pairs={{8,0},{10,2},{12,4},{14,6},{16,8},{18,10},{20,12},{22,14},{24,16},... | collective-permute-start | bytes 2359304 | tf_op jit(solution)/shard_map/ppermute | solution.py:20
  159.6 0.9 copy-start.8
  160.5 26.8 %collective-permute-start.1 = (f32[2,3,32,1024]{3,2,1,0:T(8,128)S(1)}, f32[2,3,32,1024]{3,2,1,0:T(8,128)}, u32[]{:S(2)}, u32[]{:S(2)}) collective-permute-start(f32[2,3,32,1024]{3,2,1,0:T(8,128)S(1)} %fusion.9), channel_id=1, source_target_pairs={{0,2},{2,4},{4,6},{6,8},{8,10},{10,12},{12,14},{14,16},{16,18},{18... | collective-permute-start | bytes 2359304 | tf_op jit(solution)/shard_map/ppermute | solution.py:14
  187.3 7.0 %copy-start.1 = (f32[1,3,32,1024]{3,2,1,0:T(8,128)S(1)}, f32[1,3,32,1024]{3,2,1,0:T(8,128)}, u32[]{:S(2)}) copy-start(f32[1,3,32,1024]{3,2,1,0:T(8,128)} %param.9) | copy-start | bytes 1179652
  187.3 7.0 %copy-start.2 = (f32[1,3,32,1024]{3,2,1,0:T(8,128)S(1)}, f32[1,3,32,1024]{3,2,1,0:T(8,128)}, u32[]{:S(2)}) copy-start(f32[1,3,32,1024]{3,2,1,0:T(8,128)} %param.10) | copy-start | bytes 1179652
  206.0 9.9 %copy-start.12 = (f32[32,16]{0,1:T(8,128)S(1)}, f32[32,16]{0,1:T(8,128)}, u32[]{:S(2)}) copy-start(f32[32,16]{0,1:T(8,128)} %param.15) | copy-start | bytes 6148
  206.1 10.0 %copy-start.13 = (f32[32,16]{0,1:T(8,128)S(1)}, f32[32,16]{0,1:T(8,128)}, u32[]{:S(2)}) copy-start(f32[32,16]{0,1:T(8,128)} %param.16) | copy-start | bytes 6148
  206.1 41.9 %all-to-all-start = ((f32[16,1,24576]{2,1,0:T(1,128)}), f32[16,1,24576]{2,1,0:T(1,128)S(1)}, u32[]{:S(2)}, u32[]{:S(2)}) async-start(f32[16,1,24576]{2,1,0:T(1,128)} %reshape.518), calls=%async_computation | async-start | bytes 3145728 | tf_op jit(solution)/shard_map/all_to_all | solution.py:124
  267.6 2.5 copy-start
Sparse Core Ops, SparseCore 0:
  25.4 28.5 all-gather.1
where the time goes:
time: 291 us; the launch traced here: 286 us
  waiting for transfers between devices  98.5 us (34%)
  starting transfers between devices  89.3 us (31%)
  local copies, waits for them, and re-layouts  35 us (12%)
  between operations  33.1 us (11%)
  other arithmetic  19.4 us (7%)
  matrix products  10.5 us (4%)
    ppermute x14, starting transfers between devices, from_behind(): return lax.ppermute(block, axis, route)  73.9 us
    ppermute x14, waiting for transfers between devices, from_behind(): return lax.ppermute(block, axis, route)  38.8 us
    all_to_all x1, waiting for transfers between devices, body(): lax.all_to_all(outgoing[:, None], 'sector', split_axis=4, concat_axis=1,...  31.8 us
    ppermute x2, waiting for transfers between devices, passed_along(): return lax.ppermute(value, axis, pairs)  14.9 us
    unnamed x35, local copies, waits for them, and re-layouts  14.5 us
    all_gather x1, waiting for transfers between devices, body(): gathered = lax.all_gather(relative, 'harm', axis=2, tiled=True)  13 us
    all_to_all x1, starting transfers between devices, body(): lax.all_to_all(outgoing[:, None], 'sector', split_axis=4, concat_axis=1,...  9.9 us
    all_to_all x2, local copies, waits for them, and re-layouts, body(): lax.all_to_all(outgoing[:, None], 'sector', split_axis=4, concat_axis=1,...  7.31 us
  transfers between devices with their start and end apart: 18, of which 6 were waited for; matrix products, arithmetic and copies ran while one was open for 4% of the time, Pallas kernels for 0%

commit v1 on v0

--- a/solution.py
+++ b/solution.py
@@ -2,8 +2,13 @@
 
 import jax
 import jax.numpy as jnp
+import numpy as np
 from jax import lax
+from jax.experimental import pallas as pl
+from jax.experimental.pallas import tpu as pltpu
 from jax.sharding import PartitionSpec as P
+
+MESH = pl.DeviceIdType.MESH
 
 exact_mode = lax.Precision.HIGHEST
 
@@ -74,7 +79,7 @@
     return jnp.logical_and(inside, other_group == own_group).astype(jnp.float32)[0]
 
 
-def body(
+def body_any_size(
     disp,
     direction,
     stick_state,
@@ -133,6 +138,392 @@
     return (residual, jvp)
 
 
+LANES = 128
+HALF = 64
+ROW_HARTLEY = 0
+ROW_MIRROR = 16
+ROW_SPREAD = 32
+ROW_LOAD = 48
+ROW_SAME = 176
+ROW_COEF = 304
+ROW_PICK = 432
+ROW_SQUARE = 560
+ROW_LOADS = 576
+ROW_GAPS = 704
+ROWS = 960
+
+
+def constant_table(sectors, coefs, samples):
+    k = np.arange(sectors)
+    phase = 2.0 * np.pi * (np.outer(k, k) % sectors) / sectors
+    hartley = (np.cos(phase) + np.sin(phase)) / math.sqrt(sectors)
+    out = np.zeros((ROWS, LANES), np.float64)
+    lane_sector, lane_coef = np.arange(LANES) // 8, np.arange(LANES) % 8
+    row_coef, row_k = np.arange(LANES) // sectors, np.arange(LANES) % sectors
+    out[ROW_HARTLEY : ROW_HARTLEY + 16] = hartley[:, lane_sector]
+    out[ROW_MIRROR : ROW_MIRROR + 16] = hartley[(-k) % sectors][:, lane_sector]
+    out[ROW_SPREAD : ROW_SPREAD + 16] = k[:, None] == lane_sector[None, :]
+    same = row_coef[:, None] == lane_coef[None, :]
+    reaction = hartley - np.roll(hartley, -1, 1)
+    out[ROW_LOAD : ROW_LOAD + 128] = same * reaction[row_k][:, lane_sector]
+    out[ROW_SAME : ROW_SAME + 128] = same
+    out[ROW_COEF : ROW_COEF + 128, 0:8] = row_coef[:, None] == np.arange(8)[None, :]
+    out[ROW_PICK : ROW_PICK + 128, 0:16] = row_k[:, None] == k[None, :]
+    out[ROW_SQUARE : ROW_SQUARE + 16, 0:16] = hartley
+    c, t = np.arange(coefs), np.arange(samples)
+    angle = 2.0 * np.pi * (np.outer(c // 2 + 1, t) % samples) / samples
+    basis = np.where(c[:, None] % 2 == 0, np.cos(angle), np.sin(angle))
+    for h in range(2):
+        ordered = np.roll(basis, -h * (coefs // 2), 0)
+        out[ROW_LOADS + 64 * h : ROW_LOADS + 64 * (h + 1)] = ordered * (2.0 / samples)
+        out[ROW_GAPS + 128 * h : ROW_GAPS + 128 * (h + 1), 0:64] = ordered.T
+    return out.astype(np.float32)
+
+
+def product(a, b, precision=lax.Precision.HIGH):
+    return jnp.dot(a, b, preferred_element_type=jnp.float32, precision=precision)
+
+
+def kernel(
+    disp,
+    direction,
+    states,
+    params,
+    mistuning,
+    groups,
+    diag,
+    cross,
+    excitation,
+    table,
+    residual,
+    jvp,
+    x_out,
+    s_out,
+    x_in,
+    s_in,
+    r_out,
+    r_in,
+    l_out,
+    l_in,
+    params8,
+    tractions,
+    linear,
+    x_sent,
+    x_got,
+    s_sent,
+    s_got,
+    r_sent,
+    r_got,
+    l_sent,
+    l_got,
+):
+    sectors = 16
+    pairs = sectors // 2
+    me = lax.axis_index("sector")
+    h = lax.axis_index("harm")
+    g0 = me // 2
+    partner = (me, 1 - h)
+
+    barrier = pltpu.get_barrier_semaphore()
+
+    def greet(i, carry):
+        pl.semaphore_signal(
+            barrier, inc=1, device_id=(lax.rem(me + i, sectors), h), device_id_type=MESH
+        )
+        return carry
+
+    lax.fori_loop(1, sectors, greet, 0)
+    pl.semaphore_signal(barrier, inc=1, device_id=partner, device_id_type=MESH)
+
+    def low(rows):
+        return lax.broadcasted_iota(jnp.int32, (rows, LANES), 1) < HALF
+
+    params8[0:4, :] = params[...]
+    params8[4:8, :] = params[...]
+
+    def pack(g, carry):
+        lanes = pl.ds(pl.multiple_of(g * LANES, LANES), LANES)
+        a, b = disp[:, lanes], direction[:, lanes]
+        x_out[2 * g] = jnp.where(low(96), a, pltpu.roll(b, HALF, 1))
+        x_out[2 * g + 1] = jnp.where(low(96), pltpu.roll(a, HALF, 1), b)
+        z = states[:, lanes].astype(jnp.float32)
+        early, late = z[0:64], z[64:128]
+        s_out[2 * g, 8:72, :] = jnp.where(low(64), early, pltpu.roll(late, HALF, 1))
+        s_out[2 * g + 1, 8:72, :] = jnp.where(low(64), pltpu.roll(early, HALF, 1), late)
+        p = params8[:, lanes]
+        turned = pltpu.roll(p, HALF, 1)
+        s_out[2 * g, 0:8, :] = jnp.where(low(8), p, turned)
+        s_out[2 * g + 1, 0:8, :] = jnp.where(low(8), turned, p)
+        return carry
+
+    lax.fori_loop(0, pairs, pack, 0)
+
+    def x_copy(to, source):
+        return pltpu.make_async_remote_copy(
+            src_ref=x_out.at[to],
+            dst_ref=x_in.at[source],
+            send_sem=x_sent.at[to],
+            recv_sem=x_got.at[source],
+            device_id=(to, h),
+            device_id_type=MESH,
+        )
+
+    def s_copy(to, source):
+        return pltpu.make_async_remote_copy(
+            src_ref=s_out.at[to],
+            dst_ref=s_in.at[source // 2],
+            send_sem=s_sent.at[to],
+            recv_sem=s_got.at[source // 2],
+            device_id=(to, h),
+            device_id_type=MESH,
+        )
+
+    x_in[me] = x_out[me]
+    mine_here = lax.rem(me, 2) == h
+
+    @pl.when(mine_here)
+    def _():
+        s_in[g0] = s_out[me]
+
+    pl.semaphore_wait(barrier, sectors)
+
+    def send(i, carry):
+        to = lax.rem(me + sectors - i, sectors)
+        x_copy(to, me).start()
+
+        @pl.when(mine_here)
+        def _():
+            s_copy(to, me).start()
+
+        return carry
+
+    lax.fori_loop(1, sectors, send, 0)
+
+    square = table[ROW_SQUARE : ROW_SQUARE + 16, 0:16]
+    row = lax.broadcasted_iota(jnp.int32, (16, 16), 0)
+    col = lax.broadcasted_iota(jnp.int32, (16, 16), 1)
+    group_row = jnp.broadcast_to(groups[...].astype(jnp.float32), (16, 16))
+    group_col = jnp.sum(jnp.where(row == col, group_row, 0.0), axis=1, keepdims=True)
+    together = (group_row == group_col).astype(jnp.float32)
+    mean = together / jnp.sum(together, axis=0, keepdims=True)
+    weighted = square * mistuning[...]
+    exact = lax.Precision.HIGHEST
+    tuned = weighted - product(weighted, mean, exact)
+    tuned = product(tuned, table[ROW_SPREAD : ROW_SPREAD + 16, :], exact)
+    pick = table[ROW_PICK : ROW_PICK + 128, 0:16]
+    coef_rows = table[ROW_COEF : ROW_COEF + 128, 0:8]
+    same = table[ROW_SAME : ROW_SAME + 128, :]
+    for b in range(4):
+        d = pick * product(coef_rows, diag[8 * b : 8 * b + 8, :], exact)
+        c = pick * product(coef_rows, cross[8 * b : 8 * b + 8, :], exact)
+        linear[b] = same * (
+            product(d, table[ROW_HARTLEY : ROW_HARTLEY + 16, :], exact)
+            + product(c, table[ROW_MIRROR : ROW_MIRROR + 16, :], exact)
+            + product(pick, tuned, exact)
+        )
+
+    def r_copy(j):
+        return pltpu.make_async_remote_copy(
+            src_ref=r_out.at[j],
+            dst_ref=r_in.at[j],
+            send_sem=r_sent.at[j],
+            recv_sem=r_got.at[j],
+            device_id=partner,
+            device_id_type=MESH,
+        )
+
+    def l_copy(j, sector):
+        return pltpu.make_async_remote_copy(
+            src_ref=l_out.at[j],
+            dst_ref=l_in.at[sector],
+            send_sem=l_sent.at[j],
+            recv_sem=l_got.at[sector // 2],
+            device_id=partner,
+            device_id_type=MESH,
+        )
+
+    def arrive(sector):
+        @pl.when(sector != me)
+        def _():
+            x_copy(me, sector).wait_recv()
+
+    def pair(j):
+        return lax.rem(g0 + j, pairs)
+
+    def hand_over(j):
+        g = pair(j)
+        arrive(2 * g + 1)
+
+        @pl.when(j < pairs - 1)
+        def _():
+            arrive(lax.rem(2 * g + 2, sectors))
+
+        other = 2 * g + 1 - h
+        r_out[j] = x_in[other] - x_in[lax.rem(other + 1, sectors)]
+        r_copy(j).start()
+
+    def contact(j):
+        g = pair(j)
+        sector = 2 * g + h
+        own = x_in[sector] - x_in[lax.rem(sector + 1, sectors)]
+
+        @pl.when(sector != me)
+        def _():
+            s_copy(me, sector).wait_recv()
+
+        r_copy(j).wait_recv()
+        far = r_in[j]
+        rows = [jnp.concatenate([own[32 * i : 32 * i + 32], far[32 * i : 32 * i + 32]], 0) for i in range(3)]
+        gaps_rows = pl.ds(pl.multiple_of(ROW_GAPS + 128 * h, 8), 128)
+        moved = product(table[gaps_rows, 0:64], jnp.concatenate(rows, 1))
+        law = s_in[g, 0:8, :]
+        n0, kn, kt, mu = law[0:1], law[1:2], law[2:3], law[3:4]
+        step = 32
+        for start in range(0, 128, step):
+            packed = s_in[g, 8 + start % 64 : 8 + start % 64 + step, :]
+            turned = pltpu.roll(packed, HALF, 1)
+            left = low(step)
+            z = jnp.where(left, packed, turned) if start < 64 else jnp.where(left, turned, packed)
+            raw = [moved[start : start + step, LANES * i : LANES * (i + 1)] for i in range(3)]
+            swapped = [pltpu.roll(value, HALF, 1) for value in raw]
+            gap = [jnp.where(left, u, v) for u, v in zip(raw, swapped)]
+            dgap = [jnp.where(left, v, u) for u, v in zip(raw, swapped)]
+            touching = (z < 1.5).astype(jnp.float32)
+            sliding = jnp.logical_and(z > 0.5, z < 1.5)
+            normal = (n0 + kn * gap[0]) * touching
+            dnormal = kn * dgap[0] * touching
+            inverse = lax.rsqrt(gap[1] * gap[1] + gap[2] * gap[2] + 1.0)
+            along = (gap[1] * dgap[1] + gap[2] * dgap[2]) * (inverse * inverse)
+            tractions[start : start + step, 0:LANES] = jnp.where(left, normal, dnormal)
+            rub = mu * inverse
+            for i in (1, 2):
+                slipped = normal * gap[i]
+                dslipped = dnormal * gap[i] + normal * (dgap[i] - gap[i] * along)
+                stuck = kt * raw[i] * touching
+                tractions[start : start + step, LANES * i : LANES * (i + 1)] = jnp.where(
+                    sliding, rub * jnp.where(left, slipped, dslipped), stuck
+                )
+        loads_rows = pl.ds(pl.multiple_of(ROW_LOADS + 64 * h, 8), 64)
+        loads = product(table[loads_rows, :], tractions[...])
+        for i in range(3):
+            l_out[j, 32 * i : 32 * i + 32, :] = loads[32:64, LANES * i : LANES * (i + 1)]
+        l_copy(j, sector).start()
+        for i in range(3):
+            l_in[sector, 32 * i : 32 * i + 32, :] = loads[0:32, LANES * i : LANES * (i + 1)]
+
+    arrive(2 * g0)
+    hand_over(0)
+
+    def turn(j, carry):
+        @pl.when(j < pairs - 1)
+        def _():
+            hand_over(j + 1)
+
+        contact(j)
+        return carry
+
+    lax.fori_loop(0, pairs, turn, 0)
+
+    def loads_here(j, carry):
+        l_copy(j, 2 * j + 1 - h).wait_recv()
+        return carry
+
+    lax.fori_loop(0, pairs, loads_here, 0)
+    reaction = table[ROW_LOAD : ROW_LOAD + 128, :]
+    for b in range(4):
+        matrix = jnp.concatenate([linear[b], reaction], 1)
+        columns = []
+        for i in range(3):
+            at = slice(32 * i + 8 * b, 32 * i + 8 * b + 8)
+            field = [x_in[:, at, :].reshape(128, LANES), l_in[:, at, :].reshape(128, LANES)]
+            columns.append(jnp.concatenate(field, 0))
+        out = product(matrix, jnp.concatenate(columns, 1))
+        for i in range(3):
+            both = out[:, LANES * i : LANES * (i + 1)]
+            first = both[:, 0:HALF].reshape(8, 16, HALF)
+            second = pltpu.roll(both, HALF, 1)[:, 0:HALF].reshape(8, 16, HALF)
+            residual[i, 8 * b : 8 * b + 8] = first - excitation[i, 8 * b : 8 * b + 8]
+            jvp[i, 8 * b : 8 * b + 8] = second
+
+    def sent(i, carry):
+        to = lax.rem(me + sectors - i, sectors)
+        x_copy(to, me).wait_send()
+
+        @pl.when(mine_here)
+        def _():
+            s_copy(to, me).wait_send()
+
+        return carry
+
+    lax.fori_loop(1, sectors, sent, 0)
+
+    def sent_back(j, carry):
+        r_copy(j).wait_send()
+        l_copy(j, 2 * pair(j) + h).wait_send()
+        return carry
+
+    lax.fori_loop(0, pairs, sent_back, 0)
+
+
+def body_in_kernel(
+    disp,
+    direction,
+    stick_state,
+    contact_params,
+    mistuning,
+    group_ids,
+    diag_stiff,
+    cross_stiff,
+    excitation,
+):
+    vmem = pl.BlockSpec(memory_space=pltpu.VMEM)
+    out = jax.ShapeDtypeStruct((3, 32, 16, HALF), jnp.float32)
+    dma = pltpu.SemaphoreType.DMA
+    table = jnp.asarray(constant_table(16, 64, 128))
+    residual, jvp = pl.pallas_call(
+        kernel,
+        out_shape=(out, out),
+        in_specs=[vmem] * 10,
+        out_specs=(vmem, vmem),
+        scratch_shapes=[
+            pltpu.VMEM((16, 96, LANES), jnp.float32),
+            pltpu.VMEM((16, 72, LANES), jnp.float32),
+            pltpu.VMEM((16, 96, LANES), jnp.float32),
+            pltpu.VMEM((8, 72, LANES), jnp.float32),
+            pltpu.VMEM((8, 96, LANES), jnp.float32),
+            pltpu.VMEM((8, 96, LANES), jnp.float32),
+            pltpu.VMEM((8, 96, LANES), jnp.float32),
+            pltpu.VMEM((16, 96, LANES), jnp.float32),
+            pltpu.VMEM((8, 1024), jnp.float32),
+            pltpu.VMEM((128, 3 * LANES), jnp.float32),
+            pltpu.VMEM((4, 128, LANES), jnp.float32),
+            dma((16,)),
+            dma((16,)),
+            dma((16,)),
+            dma((8,)),
+            dma((8,)),
+            dma((8,)),
+            dma((8,)),
+            dma((8,)),
+        ],
+        compiler_params=pltpu.CompilerParams(
+            collective_id=0, has_side_effects=True, vmem_limit_bytes=40 * 1024 * 1024
+        ),
+    )(
+        disp.reshape(96, 1024),
+        direction.reshape(96, 1024),
+        stick_state[0],
+        contact_params[0],
+        mistuning[None],
+        group_ids[None],
+        diag_stiff,
+        cross_stiff,
+        jnp.swapaxes(excitation, 2, 3),
+        table,
+    )
+    return (jnp.swapaxes(residual, 2, 3), jnp.swapaxes(jvp, 2, 3))
+
+
 def solution(mesh):
     in_specs = (
         P("sector", None, "harm", None),
@@ -146,4 +537,12 @@
         P(None, "harm", "sector", None),
     )
     out_specs = (P(None, "harm", "sector", None), P(None, "harm", "sector", None))
+
+    def body(*arrays):
+        _, channels, coefs, nodes = arrays[0].shape
+        sizes = (mesh.shape["sector"], mesh.shape["harm"], channels, coefs, nodes, arrays[2].shape[1])
+        if sizes == (16, 2, 3, 32, 1024, 128):
+            return body_in_kernel(*arrays)
+        return body_any_size(*arrays)
+
     return jax.shard_map(body, mesh=mesh, in_specs=in_specs, out_specs=out_specs, check_vma=False)

time: 291 us -> 58.9 us (0.20); the launches traced: 286 us -> 58.5 us
  waiting for transfers between devices: 98.5 us -> 0 us
  starting transfers between devices: 89.3 us -> 0 us
  Pallas kernels: 0 us -> 48.8 us
  between operations: 33.1 us -> 0.66 us
  local copies, waits for them, and re-layouts: 35 us -> 9.06 us
  other arithmetic: 19.4 us -> 0 us
  matrix products: 10.5 us -> 0 us
    ppermute x16 -> x0, starting transfers between devices: 79.4 us -> none  [the longest x14 73.9 us: from_behind(): return lax.ppermute(block, axis, route)]
    ppermute x16 -> x0, waiting for transfers between devices: 53.7 us -> none  [the longest x14 38.8 us: from_behind(): return lax.ppermute(block, axis, route)]
    pallas_call x0 -> x1, Pallas kernels: none -> 48.8 us  [body_in_kernel(): pl.pallas_call(kernel, out_shape=(out, out), in_specs=[vmem] * 10, out_sp...]
    all_to_all x1 -> x0, waiting for transfers between devices: 31.8 us -> none  [body(): lax.all_to_all(outgoing[:, None], 'sector', split_axis=4, concat_axis=1,...]
    all_gather x1 -> x0, waiting for transfers between devices: 13 us -> none  [body(): gathered = lax.all_gather(relative, 'harm', axis=2, tiled=True)]
    dot_general x4 -> x0, matrix products: 10.5 us -> none  [the longest x1 4.35 us: body(): gaps = jnp.einsum('wcjp,jt->wctp', gathered, table, precision=exact_mode)]
    add x2 -> x0, other arithmetic: 10.3 us -> none  [the longest x1 7.01 us: body(): forces = loads - earlier_loads + weight * (paired - totals / members)]
    all_to_all x1 -> x0, starting transfers between devices: 9.9 us -> none  [body(): lax.all_to_all(outgoing[:, None], 'sector', split_axis=4, concat_axis=1,...]
  transfers between devices with their start and end apart: 18 -> 0, of which waited for: 6 -> 0; matrix products, arithmetic and copies ran while one was open for 4% -> 0% of each run, Pallas kernels for 0% -> 0%
where the time goes in v1:
time: 58.9 us; the launch traced here: 58.5 us
  Pallas kernels  48.8 us (83%)
  local copies, waits for them, and re-layouts  9.06 us (15%)
  between operations  0.66 us (1%)
    pallas_call x1, Pallas kernels, body_in_kernel(): pl.pallas_call(kernel, out_shape=(out, out), in_specs=[vmem] * 10, out_sp...  48.8 us
    unnamed x24, local copies, waits for them, and re-layouts  9.06 us

profile of v1, /device:TPU:0, one launch (start us, length us, event | category | flops | bytes accessed | tf_op | source)
XLA Modules:
  0.0 58.5 jit_solution(14009306753399702319)
XLA Ops:
  0.6 0.0 copy-start.8
  0.6 0.7 %copy-done.8 = f32[32,16]{0,1:T(8,128)S(1)} copy-done((f32[32,16]{0,1:T(8,128)S(1)}, f32[32,16]{0,1:T(8,128)}, u32[]{:S(2)}) %copy-start.8) | copy-done | bytes 2072
  1.3 0.0 copy-start.9
  1.3 0.1 copy.12.diag
  1.4 0.6 %copy-done.9 = f32[32,16]{0,1:T(8,128)S(1)} copy-done((f32[32,16]{0,1:T(8,128)S(1)}, f32[32,16]{0,1:T(8,128)}, u32[]{:S(2)}) %copy-start.9) | copy-done | bytes 2072
  2.0 0.0 copy-start.5
  2.0 0.0 copy-start.6
  2.0 0.0 copy-start.7
  2.0 0.1 copy.13.cross
  2.1 0.6 %copy-done.5 = f32[1,4,1024]{2,1,0:T(4,128)S(1)} copy-done((f32[1,4,1024]{2,1,0:T(4,128)S(1)}, f32[1,4,1024]{2,1,0:T(4,128)}, u32[]{:S(2)}) %copy-start.5) | copy-done | bytes 16408
  2.7 0.0 copy-done.6
  2.7 0.0 copy-done.7
  2.7 0.0 copy-start
  2.8 1.1 %copy-done = f32[3,32,64,16]{2,3,1,0:T(8,128)S(1)} copy-done((f32[3,32,64,16]{2,3,1,0:T(8,128)S(1)}, f32[3,32,64,16]{2,3,1,0:T(8,128)}, u32[]{:S(2)}) %copy-start) | copy-done | bytes 393240
  3.9 0.0 copy-start.1
  3.9 1.0 %copy-done.1 = s32[1,128,1024]{2,1,0:T(8,128)S(1)} copy-done((s32[1,128,1024]{2,1,0:T(8,128)S(1)}, s32[1,128,1024]{2,1,0:T(8,128)}, u32[]{:S(2)}) %copy-start.1) | copy-done | bytes 524312
  4.9 0.0 copy-start.2
  4.9 1.0 %copy-done.2 = f32[960,128]{1,0:T(8,128)S(1)} copy-done((f32[960,128]{1,0:T(8,128)S(1)}, f32[960,128]{1,0:T(8,128)}, u32[]{:S(2)}) %copy-start.2) | copy-done | bytes 491544
  6.0 0.0 copy-start.3
  6.0 1.0 %copy-done.3 = f32[1,3,32,1024]{3,2,1,0:T(8,128)S(1)} copy-done((f32[1,3,32,1024]{3,2,1,0:T(8,128)S(1)}, f32[1,3,32,1024]{3,2,1,0:T(8,128)}, u32[]{:S(2)}) %copy-start.3) | copy-done | bytes 393240
  7.0 0.0 copy-start.4
  7.0 1.0 %copy-done.4 = f32[1,3,32,1024]{3,2,1,0:T(8,128)S(1)} copy-done((f32[1,3,32,1024]{3,2,1,0:T(8,128)S(1)}, f32[1,3,32,1024]{3,2,1,0:T(8,128)}, u32[]{:S(2)}) %copy-start.4) | copy-done | bytes 393240
  7.9 48.8 %shard_map.113 = (f32[3,32,16,64]{3,2,1,0:T(8,128)S(1)}, f32[3,32,16,64]{3,2,1,0:T(8,128)S(1)}) custom-call(f32[96,1024]{1,0:T(8,128)S(1)} %bitcast.13, f32[96,1024]{1,0:T(8,128)S(1)} %bitcast.14, s32[128,1024]{1,0:T(8,128)S(1)} %bitcast.12, f32[4,1024]{1,0:T(4,128)S(1)} %bitcast.15, f32[1,16]{1,0:T(1,128)S(1)} %bitcast.16, s32[1,16]{1,0:T(1,128)S(1)} %bitcast.17, ...), custom_call_target="tpu_custom_call" | custom-call | tf_op jit(solution)/shard_map/pallas_call | solution.py:483
  56.7 0.9 %copy.16 = f32[3,32,64,16]{2,3,1,0:T(8,128)} copy(f32[3,32,64,16]{2,3,1,0:T(8,128)S(1)} %bitcast.10) | data formatting | bytes 786432
  57.6 0.9 %copy.17 = f32[3,32,64,16]{2,3,1,0:T(8,128)} copy(f32[3,32,64,16]{2,3,1,0:T(8,128)S(1)} %bitcast.9) | data formatting | bytes 786432
Async XLA Ops:
  0.6 0.7 %copy-start.8 = (f32[32,16]{0,1:T(8,128)S(1)}, f32[32,16]{0,1:T(8,128)}, u32[]{:S(2)}) copy-start(f32[32,16]{0,1:T(8,128)} %param.16) | copy-start | bytes 6148
  1.3 0.7 %copy-start.9 = (f32[32,16]{0,1:T(8,128)S(1)}, f32[32,16]{0,1:T(8,128)}, u32[]{:S(2)}) copy-start(f32[32,16]{0,1:T(8,128)} %param.17) | copy-start | bytes 6148
  2.0 0.7 %copy-start.5 = (f32[1,4,1024]{2,1,0:T(4,128)S(1)}, f32[1,4,1024]{2,1,0:T(4,128)}, u32[]{:S(2)}) copy-start(f32[1,4,1024]{2,1,0:T(4,128)} %param.13) | copy-start | bytes 49156
  2.0 0.7 %copy-start.6 = (f32[16]{0:T(128)S(1)}, f32[16]{0:T(128)}, u32[]{:S(2)}) copy-start(f32[16]{0:T(128)} %param.14) | copy-start | bytes 196
  2.0 0.7 %copy-start.7 = (s32[16]{0:T(128)S(1)}, s32[16]{0:T(128)}, u32[]{:S(2)}) copy-start(s32[16]{0:T(128)} %param.15) | copy-start | bytes 196
  2.7 1.1 %copy-start = (f32[3,32,64,16]{2,3,1,0:T(8,128)S(1)}, f32[3,32,64,16]{2,3,1,0:T(8,128)}, u32[]{:S(2)}) copy-start(f32[3,32,64,16]{2,3,1,0:T(8,128)} %param.18) | copy-start | bytes 1179652
  3.9 1.0 %copy-start.1 = (s32[1,128,1024]{2,1,0:T(8,128)S(1)}, s32[1,128,1024]{2,1,0:T(8,128)}, u32[]{:S(2)}) copy-start(s32[1,128,1024]{2,1,0:T(8,128)} %param.12) | copy-start | bytes 1572868
  4.9 1.0 %copy-start.2 = (f32[960,128]{1,0:T(8,128)S(1)}, f32[960,128]{1,0:T(8,128)}, u32[]{:S(2)}) copy-start(f32[960,128]{1,0:T(8,128)} %constant.2.clone.table) | copy-start | bytes 1474564
  6.0 1.0 %copy-start.3 = (f32[1,3,32,1024]{3,2,1,0:T(8,128)S(1)}, f32[1,3,32,1024]{3,2,1,0:T(8,128)}, u32[]{:S(2)}) copy-start(f32[1,3,32,1024]{3,2,1,0:T(8,128)} %param.10) | copy-start | bytes 1179652
  7.0 1.0 %copy-start.4 = (f32[1,3,32,1024]{3,2,1,0:T(8,128)S(1)}, f32[1,3,32,1024]{3,2,1,0:T(8,128)}, u32[]{:S(2)}) copy-start(f32[1,3,32,1024]{3,2,1,0:T(8,128)} %param.11) | copy-start | bytes 1179652

commit v2 on v1

--- a/solution.py
+++ b/solution.py
@@ -184,7 +184,33 @@
     return jnp.dot(a, b, preferred_element_type=jnp.float32, precision=precision)
 
 
+SEND_ORDER = ((0, 2, 3, 1), (1, 0, 2, 3), (2, 3, 1, 0), (3, 1, 0, 2))
+PAIR_ORDER = (
+    (0, 1, 2, 6, 7, 3, 4, 5),
+    (2, 6, 7, 0, 1, 3, 4, 5),
+    (4, 0, 5, 6, 7, 1, 2, 3),
+    (6, 4, 5, 7, 0, 1, 2, 3),
+)
+
+
+def seen(z, k, step):
+    order = PAIR_ORDER[z]
+    return int((order[k] + step) % 8 not in order[:k])
+
+
 def kernel(
+    disp_hbm,
+    direction_hbm,
+    states_hbm,
+    params_hbm,
+    mistuning_hbm,
+    groups_hbm,
+    diag_hbm,
+    cross_hbm,
+    excitation_hbm,
+    table_hbm,
+    residual,
+    jvp,
     disp,
     direction,
     states,
@@ -195,8 +221,7 @@
     cross,
     excitation,
     table,
-    residual,
-    jvp,
+    fetched,
     x_out,
     s_out,
     x_in,
@@ -222,7 +247,28 @@
     me = lax.axis_index("sector")
     h = lax.axis_index("harm")
     g0 = me // 2
+    z0 = me // 4
     partner = (me, 1 - h)
+
+    given = (
+        disp_hbm,
+        direction_hbm,
+        states_hbm,
+        params_hbm,
+        mistuning_hbm,
+        groups_hbm,
+        diag_hbm,
+        cross_hbm,
+        excitation_hbm,
+        table_hbm,
+    )
+    held = (disp, direction, states, params, mistuning, groups, diag, cross, excitation, table)
+    fetches = [
+        pltpu.make_async_copy(source, target, fetched.at[i])
+        for i, (source, target) in enumerate(zip(given, held))
+    ]
+    for fetch in fetches:
+        fetch.start()
 
     barrier = pltpu.get_barrier_semaphore()
 
@@ -235,9 +281,28 @@
     lax.fori_loop(1, sectors, greet, 0)
     pl.semaphore_signal(barrier, inc=1, device_id=partner, device_id_type=MESH)
 
+    def by_z(values):
+        out = jnp.int32(values[3])
+        for z in (2, 1, 0):
+            out = jnp.where(z0 == z, values[z], out)
+        return out
+
+    def at_step(column, j):
+        out = column[-1]
+        for k in range(len(column) - 2, -1, -1):
+            out = jnp.where(j == k, column[k], out)
+        return out
+
+    send_order = [by_z([SEND_ORDER[z][k] for z in range(4)]) for k in range(4)]
+    pair_order = [by_z([PAIR_ORDER[z][k] for z in range(4)]) for k in range(8)]
+    new_first = [by_z([seen(z, k, -1) for z in range(4)]) for k in range(8)]
+    new_last = [by_z([seen(z, k, 1) for z in range(4)]) for k in range(8)]
+
     def low(rows):
         return lax.broadcasted_iota(jnp.int32, (rows, LANES), 1) < HALF
 
+    for i in range(4):
+        fetches[i].wait()
     params8[0:4, :] = params[...]
     params8[4:8, :] = params[...]
 
@@ -286,18 +351,26 @@
         s_in[g0] = s_out[me]
 
     pl.semaphore_wait(barrier, sectors)
+    core, x = lax.rem(me, 2), lax.rem(g0, 2)
 
     def send(i, carry):
-        to = lax.rem(me + sectors - i, sectors)
-        x_copy(to, me).start()
-
-        @pl.when(mine_here)
+        z = at_step(send_order, i // 4)
+        q = lax.rem(i, 4)
+        to = 4 * z + 2 * lax.rem(q + core, 2) + lax.rem(q // 2 + x, 2)
+
+        @pl.when(to != me)
         def _():
-            s_copy(to, me).start()
+            x_copy(to, me).start()
+
+            @pl.when(mine_here)
+            def _():
+                s_copy(to, me).start()
 
         return carry
 
-    lax.fori_loop(1, sectors, send, 0)
+    lax.fori_loop(0, sectors, send, 0)
+    for i in range(4, 10):
+        fetches[i].wait()
 
     square = table[ROW_SQUARE : ROW_SQUARE + 16, 0:16]
     row = lax.broadcasted_iota(jnp.int32, (16, 16), 0)
@@ -311,16 +384,19 @@
     tuned = weighted - product(weighted, mean, exact)
     tuned = product(tuned, table[ROW_SPREAD : ROW_SPREAD + 16, :], exact)
     pick = table[ROW_PICK : ROW_PICK + 128, 0:16]
-    coef_rows = table[ROW_COEF : ROW_COEF + 128, 0:8]
     same = table[ROW_SAME : ROW_SAME + 128, :]
+    plain = product(pick, table[ROW_HARTLEY : ROW_HARTLEY + 16, :], exact)
+    turned_back = product(pick, table[ROW_MIRROR : ROW_MIRROR + 16, :], exact)
+    tuned = product(pick, tuned, exact)
+    diag_rows = product(pick, diag[...], exact)
+    cross_rows = product(pick, cross[...], exact)
+    coef_here = lax.broadcasted_iota(jnp.int32, (128, 32), 0) // 16
+    coef_lane = lax.broadcasted_iota(jnp.int32, (128, 32), 1)
     for b in range(4):
-        d = pick * product(coef_rows, diag[8 * b : 8 * b + 8, :], exact)
-        c = pick * product(coef_rows, cross[8 * b : 8 * b + 8, :], exact)
-        linear[b] = same * (
-            product(d, table[ROW_HARTLEY : ROW_HARTLEY + 16, :], exact)
-            + product(c, table[ROW_MIRROR : ROW_MIRROR + 16, :], exact)
-            + product(pick, tuned, exact)
-        )
+        chosen = coef_lane == coef_here + 8 * b
+        d = jnp.sum(jnp.where(chosen, diag_rows, 0.0), axis=1, keepdims=True)
+        c = jnp.sum(jnp.where(chosen, cross_rows, 0.0), axis=1, keepdims=True)
+        linear[b] = same * (d * plain + c * turned_back + tuned)
 
     def r_copy(j):
         return pltpu.make_async_remote_copy(
@@ -348,13 +424,17 @@
             x_copy(me, sector).wait_recv()
 
     def pair(j):
-        return lax.rem(g0 + j, pairs)
+        return at_step(pair_order, j)
 
     def hand_over(j):
         g = pair(j)
         arrive(2 * g + 1)
 
-        @pl.when(j < pairs - 1)
+        @pl.when(at_step(new_first, j) == 1)
+        def _():
+            arrive(2 * g)
+
+        @pl.when(at_step(new_last, j) == 1)
         def _():
             arrive(lax.rem(2 * g + 2, sectors))
 
@@ -411,8 +491,7 @@
         for i in range(3):
             l_in[sector, 32 * i : 32 * i + 32, :] = loads[0:32, LANES * i : LANES * (i + 1)]
 
-    arrive(2 * g0)
-    hand_over(0)
+    hand_over(jnp.int32(0))
 
     def turn(j, carry):
         @pl.when(j < pairs - 1)
@@ -446,7 +525,7 @@
             jvp[i, 8 * b : 8 * b + 8] = second
 
     def sent(i, carry):
-        to = lax.rem(me + sectors - i, sectors)
+        to = lax.rem(me + i, sectors)
         x_copy(to, me).wait_send()
 
         @pl.when(mine_here)
@@ -477,15 +556,27 @@
     excitation,
 ):
     vmem = pl.BlockSpec(memory_space=pltpu.VMEM)
+    hbm = pl.BlockSpec(memory_space=pltpu.HBM)
     out = jax.ShapeDtypeStruct((3, 32, 16, HALF), jnp.float32)
     dma = pltpu.SemaphoreType.DMA
     table = jnp.asarray(constant_table(16, 64, 128))
     residual, jvp = pl.pallas_call(
         kernel,
         out_shape=(out, out),
-        in_specs=[vmem] * 10,
+        in_specs=[hbm] * 10,
         out_specs=(vmem, vmem),
         scratch_shapes=[
+            pltpu.VMEM((96, 1024), jnp.float32),
+            pltpu.VMEM((96, 1024), jnp.float32),
+            pltpu.VMEM((128, 1024), jnp.int32),
+            pltpu.VMEM((4, 1024), jnp.float32),
+            pltpu.VMEM((1, 16), jnp.float32),
+            pltpu.VMEM((1, 16), jnp.int32),
+            pltpu.VMEM((16, 32), jnp.float32),
+            pltpu.VMEM((16, 32), jnp.float32),
+            pltpu.VMEM((3, 32, 16, HALF), jnp.float32),
+            pltpu.VMEM((ROWS, LANES), jnp.float32),
+            dma((10,)),
             pltpu.VMEM((16, 96, LANES), jnp.float32),
             pltpu.VMEM((16, 72, LANES), jnp.float32),
             pltpu.VMEM((16, 96, LANES), jnp.float32),
@@ -507,7 +598,7 @@
             dma((8,)),
         ],
         compiler_params=pltpu.CompilerParams(
-            collective_id=0, has_side_effects=True, vmem_limit_bytes=40 * 1024 * 1024
+            collective_id=0, has_side_effects=True, vmem_limit_bytes=63 * 1024 * 1024
         ),
     )(
         disp.reshape(96, 1024),
@@ -516,8 +607,8 @@
         contact_params[0],
         mistuning[None],
         group_ids[None],
-        diag_stiff,
-        cross_stiff,
+        diag_stiff.T,
+        cross_stiff.T,
         jnp.swapaxes(excitation, 2, 3),
         table,
     )

time: 58.9 us -> 46.4 us (0.79)
  Pallas kernels: 48.8 us -> 42.6 us
  local copies, waits for them, and re-layouts: 9.06 us -> 3.02 us
    pallas_call x1, Pallas kernels: 48.8 us -> 42.6 us  [body_in_kernel(): pl.pallas_call(kernel, out_shape=(out, out), in_specs=[hbm] * 10, out_spe...]
    unnamed x24 -> x4, local copies, waits for them, and re-layouts: 9.06 us -> 3.02 us
where the time goes in v2:
time: 46.4 us; the launch traced here: 46.3 us
  Pallas kernels  42.6 us (92%)
  local copies, waits for them, and re-layouts  3.02 us (7%)
  between operations  0.65 us (1%)
    pallas_call x1, Pallas kernels, body_in_kernel(): pl.pallas_call(kernel, out_shape=(out, out), in_specs=[hbm] * 10, out_spe...  42.6 us
    unnamed x4, local copies, waits for them, and re-layouts  3.02 us

profile of v2, /device:TPU:0, one launch (start us, length us, event | category | flops | bytes accessed | tf_op | source)
XLA Modules:
  0.0 46.3 jit_solution(14803796738573745994)
XLA Ops:
  0.6 42.6 %shard_map.113 = (f32[3,32,16,64]{3,2,1,0:T(8,128)}, f32[3,32,16,64]{3,2,1,0:T(8,128)}) custom-call(f32[96,1024]{1,0:T(8,128)} %bitcast.15, f32[96,1024]{1,0:T(8,128)} %bitcast.16, s32[128,1024]{1,0:T(8,128)} %bitcast.14, f32[4,1024]{1,0:T(4,128)} %bitcast.17, f32[1,16]{1,0:T(1,128)} %bitcast.20, s32[1,16]{1,0:T(1,128)} %bitcast.21, f32[16,32]{1,0:T(8,128)} %bitcast.18, ...), custom_call_target="tpu_custom_call" | custom-call | tf_op jit(solution)/shard_map/pallas_call | solution.py:563
  43.2 0.0 copy-start
  43.3 2.1 %copy.14 = f32[3,32,64,16]{2,3,1,0:T(8,128)} copy(f32[3,32,64,16]{2,3,1,0:T(8,128)} %bitcast.12) | data formatting | bytes 786432
  45.4 0.0 copy-done
  45.4 0.9 %copy.15 = f32[3,32,64,16]{2,3,1,0:T(8,128)} copy(f32[3,32,64,16]{2,3,1,0:T(8,128)S(1)} %bitcast.11) | data formatting | bytes 786432
Async XLA Ops:
  43.2 2.1 %copy-start = (f32[3,32,16,64]{3,2,1,0:T(8,128)S(1)}, f32[3,32,16,64]{3,2,1,0:T(8,128)}, u32[]{:S(2)}) copy-start(f32[3,32,16,64]{3,2,1,0:T(8,128)} %get-tuple-element.5) | copy-start | bytes 1179652

commit v3 on v2

--- a/solution.py
+++ b/solution.py
@@ -139,6 +139,7 @@
 
 
 LANES = 128
+VMEM_KERNEL = 63 * 1024 * 1024
 HALF = 64
 ROW_HARTLEY = 0
 ROW_MIRROR = 16
@@ -184,7 +185,7 @@
     return jnp.dot(a, b, preferred_element_type=jnp.float32, precision=precision)
 
 
-SEND_ORDER = ((0, 2, 3, 1), (1, 0, 2, 3), (2, 3, 1, 0), (3, 1, 0, 2))
+SEND_ORDER = ((2, 0, 3, 1), (0, 1, 2, 3), (3, 2, 1, 0), (1, 3, 0, 2))
 PAIR_ORDER = (
     (0, 1, 2, 6, 7, 3, 4, 5),
     (2, 6, 7, 0, 1, 3, 4, 5),
@@ -207,10 +208,10 @@
     groups_hbm,
     diag_hbm,
     cross_hbm,
-    excitation_hbm,
     table_hbm,
-    residual,
-    jvp,
+    x_hbm,
+    l_hbm,
+    linear_hbm,
     disp,
     direction,
     states,
@@ -219,9 +220,9 @@
     groups,
     diag,
     cross,
-    excitation,
     table,
     fetched,
+    fetched_parts,
     x_out,
     s_out,
     x_in,
@@ -233,6 +234,9 @@
     params8,
     tractions,
     linear,
+    x_kept,
+    l_kept,
+    linear_kept,
     x_sent,
     x_got,
     s_sent,
@@ -250,24 +254,42 @@
     z0 = me // 4
     partner = (me, 1 - h)
 
-    given = (
-        disp_hbm,
-        direction_hbm,
-        states_hbm,
-        params_hbm,
-        mistuning_hbm,
-        groups_hbm,
-        diag_hbm,
-        cross_hbm,
-        excitation_hbm,
-        table_hbm,
-    )
-    held = (disp, direction, states, params, mistuning, groups, diag, cross, excitation, table)
+    def by_z(values):
+        out = jnp.int32(values[3])
+        for z in (2, 1, 0):
+            out = jnp.where(z0 == z, values[z], out)
+        return out
+
+    def at_step(column, j):
+        out = column[-1]
+        for k in range(len(column) - 2, -1, -1):
+            out = jnp.where(j == k, column[k], out)
+        return out
+
+    send_order = [by_z([SEND_ORDER[z][k] for z in range(4)]) for k in range(4)]
+    pair_order = [by_z([PAIR_ORDER[z][k] for z in range(4)]) for k in range(8)]
+    new_first = [by_z([seen(z, k, -1) for z in range(4)]) for k in range(8)]
+    new_last = [by_z([seen(z, k, 1) for z in range(4)]) for k in range(8)]
+
+    def part(i, z):
+        lanes = pl.ds(pl.multiple_of(z * 2 * LANES, 2 * LANES), 2 * LANES)
+        source, target = ((disp_hbm, disp), (direction_hbm, direction), (states_hbm, states))[i]
+        return pltpu.make_async_copy(
+            source.at[:, lanes], target.at[:, lanes], fetched_parts.at[i, z]
+        )
+
+    given = (params_hbm, mistuning_hbm, groups_hbm, diag_hbm, cross_hbm, table_hbm)
+    held = (params, mistuning, groups, diag, cross, table)
     fetches = [
         pltpu.make_async_copy(source, target, fetched.at[i])
         for i, (source, target) in enumerate(zip(given, held))
     ]
-    for fetch in fetches:
+    for k in range(4):
+        for i in range(3):
+            part(i, send_order[k]).start()
+        if k == 0:
+            fetches[0].start()
+    for fetch in fetches[1:]:
         fetch.start()
 
     barrier = pltpu.get_barrier_semaphore()
@@ -281,32 +303,10 @@
     lax.fori_loop(1, sectors, greet, 0)
     pl.semaphore_signal(barrier, inc=1, device_id=partner, device_id_type=MESH)
 
-    def by_z(values):
-        out = jnp.int32(values[3])
-        for z in (2, 1, 0):
-            out = jnp.where(z0 == z, values[z], out)
-        return out
-
-    def at_step(column, j):
-        out = column[-1]
-        for k in range(len(column) - 2, -1, -1):
-            out = jnp.where(j == k, column[k], out)
-        return out
-
-    send_order = [by_z([SEND_ORDER[z][k] for z in range(4)]) for k in range(4)]
-    pair_order = [by_z([PAIR_ORDER[z][k] for z in range(4)]) for k in range(8)]
-    new_first = [by_z([seen(z, k, -1) for z in range(4)]) for k in range(8)]
-    new_last = [by_z([seen(z, k, 1) for z in range(4)]) for k in range(8)]
-
     def low(rows):
         return lax.broadcasted_iota(jnp.int32, (rows, LANES), 1) < HALF
 
-    for i in range(4):
-        fetches[i].wait()
-    params8[0:4, :] = params[...]
-    params8[4:8, :] = params[...]
-
-    def pack(g, carry):
+    def pack(g):
         lanes = pl.ds(pl.multiple_of(g * LANES, LANES), LANES)
         a, b = disp[:, lanes], direction[:, lanes]
         x_out[2 * g] = jnp.where(low(96), a, pltpu.roll(b, HALF, 1))
@@ -319,9 +319,6 @@
         turned = pltpu.roll(p, HALF, 1)
         s_out[2 * g, 0:8, :] = jnp.where(low(8), p, turned)
         s_out[2 * g + 1, 0:8, :] = jnp.where(low(8), turned, p)
-        return carry
-
-    lax.fori_loop(0, pairs, pack, 0)
 
     def x_copy(to, source):
         return pltpu.make_async_remote_copy(
@@ -343,34 +340,51 @@
             device_id_type=MESH,
         )
 
-    x_in[me] = x_out[me]
     mine_here = lax.rem(me, 2) == h
-
-    @pl.when(mine_here)
-    def _():
-        s_in[g0] = s_out[me]
-
-    pl.semaphore_wait(barrier, sectors)
     core, x = lax.rem(me, 2), lax.rem(g0, 2)
 
-    def send(i, carry):
-        z = at_step(send_order, i // 4)
-        q = lax.rem(i, 4)
-        to = 4 * z + 2 * lax.rem(q + core, 2) + lax.rem(q // 2 + x, 2)
-
-        @pl.when(to != me)
-        def _():
-            x_copy(to, me).start()
+    def send(k, carry):
+        z = at_step(send_order, k)
+        for i in range(3):
+            part(i, z).wait()
+
+        @pl.when(k == 0)
+        def _():
+            fetches[0].wait()
+            params8[0:4, :] = params[...]
+            params8[4:8, :] = params[...]
+
+        pack(2 * z)
+        pack(2 * z + 1)
+
+        @pl.when(k == 0)
+        def _():
+            pl.semaphore_wait(barrier, sectors)
+
+        @pl.when(z == z0)
+        def _():
+            x_in[me] = x_out[me]
 
             @pl.when(mine_here)
             def _():
-                s_copy(to, me).start()
+                s_in[g0] = s_out[me]
+
+        for q in range(4):
+            to = 4 * z + 2 * lax.rem(q + core, 2) + lax.rem(q // 2 + x, 2)
+
+            @pl.when(to != me)
+            def _():
+                x_copy(to, me).start()
+
+                @pl.when(mine_here)
+                def _():
+                    s_copy(to, me).start()
 
         return carry
 
-    lax.fori_loop(0, sectors, send, 0)
-    for i in range(4, 10):
-        fetches[i].wait()
+    lax.fori_loop(0, 4, send, 0)
+    for fetch in fetches[1:]:
+        fetch.wait()
 
     square = table[ROW_SQUARE : ROW_SQUARE + 16, 0:16]
     row = lax.broadcasted_iota(jnp.int32, (16, 16), 0)
@@ -397,6 +411,13 @@
         d = jnp.sum(jnp.where(chosen, diag_rows, 0.0), axis=1, keepdims=True)
         c = jnp.sum(jnp.where(chosen, cross_rows, 0.0), axis=1, keepdims=True)
         linear[b] = same * (d * plain + c * turned_back + tuned)
+
+    linear_copy = pltpu.make_async_copy(linear, linear_hbm, linear_kept)
+    linear_copy.start()
+    x_keep = pltpu.make_async_copy(x_in, x_hbm, x_kept)
+
+    def l_keep(sector):
+        return pltpu.make_async_copy(l_in.at[sector], l_hbm.at[sector], l_kept.at[sector])
 
     def r_copy(j):
         return pltpu.make_async_remote_copy(
@@ -490,6 +511,7 @@
         l_copy(j, sector).start()
         for i in range(3):
             l_in[sector, 32 * i : 32 * i + 32, :] = loads[0:32, LANES * i : LANES * (i + 1)]
+        l_keep(sector).start()
 
     hand_over(jnp.int32(0))
 
@@ -498,31 +520,22 @@
         def _():
             hand_over(j + 1)
 
+        @pl.when(j == pairs - 2)
+        def _():
+            x_keep.start()
+
         contact(j)
         return carry
 
     lax.fori_loop(0, pairs, turn, 0)
 
     def loads_here(j, carry):
-        l_copy(j, 2 * j + 1 - h).wait_recv()
+        sector = 2 * pair(j) + 1 - h
+        l_copy(j, sector).wait_recv()
+        l_keep(sector).start()
         return carry
 
     lax.fori_loop(0, pairs, loads_here, 0)
-    reaction = table[ROW_LOAD : ROW_LOAD + 128, :]
-    for b in range(4):
-        matrix = jnp.concatenate([linear[b], reaction], 1)
-        columns = []
-        for i in range(3):
-            at = slice(32 * i + 8 * b, 32 * i + 8 * b + 8)
-            field = [x_in[:, at, :].reshape(128, LANES), l_in[:, at, :].reshape(128, LANES)]
-            columns.append(jnp.concatenate(field, 0))
-        out = product(matrix, jnp.concatenate(columns, 1))
-        for i in range(3):
-            both = out[:, LANES * i : LANES * (i + 1)]
-            first = both[:, 0:HALF].reshape(8, 16, HALF)
-            second = pltpu.roll(both, HALF, 1)[:, 0:HALF].reshape(8, 16, HALF)
-            residual[i, 8 * b : 8 * b + 8] = first - excitation[i, 8 * b : 8 * b + 8]
-            jvp[i, 8 * b : 8 * b + 8] = second
 
     def sent(i, carry):
         to = lax.rem(me + i, sectors)
@@ -542,6 +555,29 @@
         return carry
 
     lax.fori_loop(0, pairs, sent_back, 0)
+    linear_copy.wait()
+    x_keep.wait()
+
+    def kept(i, carry):
+        l_keep(i).wait()
+        return carry
+
+    lax.fori_loop(0, sectors, kept, 0)
+
+
+def to_diameters(x_in, l_in, linear, reaction, excitation, residual, jvp):
+    matrix = jnp.concatenate([linear[0], reaction[...]], 1)
+    columns = []
+    for i in range(3):
+        field = [x_in[:, i].reshape(128, LANES), l_in[:, i].reshape(128, LANES)]
+        columns.append(jnp.concatenate(field, 0))
+    out = product(matrix, jnp.concatenate(columns, 1), lax.Precision.HIGH)
+    for i in range(3):
+        both = out[:, LANES * i : LANES * (i + 1)]
+        first = both[:, 0:HALF].reshape(8, 16, HALF)
+        second = pltpu.roll(both, HALF, 1)[:, 0:HALF].reshape(8, 16, HALF)
+        residual[i] = first - excitation[i]
+        jvp[i] = second
 
 
 def body_in_kernel(
@@ -555,39 +591,45 @@
     cross_stiff,
     excitation,
 ):
-    vmem = pl.BlockSpec(memory_space=pltpu.VMEM)
     hbm = pl.BlockSpec(memory_space=pltpu.HBM)
-    out = jax.ShapeDtypeStruct((3, 32, 16, HALF), jnp.float32)
     dma = pltpu.SemaphoreType.DMA
-    table = jnp.asarray(constant_table(16, 64, 128))
-    residual, jvp = pl.pallas_call(
+    f32 = jnp.float32
+    table = constant_table(16, 64, 128)
+    x_in, l_in, linear = pl.pallas_call(
         kernel,
-        out_shape=(out, out),
-        in_specs=[hbm] * 10,
-        out_specs=(vmem, vmem),
+        out_shape=(
+            jax.ShapeDtypeStruct((16, 96, LANES), f32),
+            jax.ShapeDtypeStruct((16, 96, LANES), f32),
+            jax.ShapeDtypeStruct((4, 128, LANES), f32),
+        ),
+        in_specs=[hbm] * 9,
+        out_specs=(hbm, hbm, hbm),
         scratch_shapes=[
-            pltpu.VMEM((96, 1024), jnp.float32),
-            pltpu.VMEM((96, 1024), jnp.float32),
+            pltpu.VMEM((96, 1024), f32),
+            pltpu.VMEM((96, 1024), f32),
             pltpu.VMEM((128, 1024), jnp.int32),
-            pltpu.VMEM((4, 1024), jnp.float32),
-            pltpu.VMEM((1, 16), jnp.float32),
+            pltpu.VMEM((4, 1024), f32),
+            pltpu.VMEM((1, 16), f32),
             pltpu.VMEM((1, 16), jnp.int32),
-            pltpu.VMEM((16, 32), jnp.float32),
-            pltpu.VMEM((16, 32), jnp.float32),
-            pltpu.VMEM((3, 32, 16, HALF), jnp.float32),
-            pltpu.VMEM((ROWS, LANES), jnp.float32),
-            dma((10,)),
-            pltpu.VMEM((16, 96, LANES), jnp.float32),
-            pltpu.VMEM((16, 72, LANES), jnp.float32),
-            pltpu.VMEM((16, 96, LANES), jnp.float32),
-            pltpu.VMEM((8, 72, LANES), jnp.float32),
-            pltpu.VMEM((8, 96, LANES), jnp.float32),
-            pltpu.VMEM((8, 96, LANES), jnp.float32),
-            pltpu.VMEM((8, 96, LANES), jnp.float32),
-            pltpu.VMEM((16, 96, LANES), jnp.float32),
-            pltpu.VMEM((8, 1024), jnp.float32),
-            pltpu.VMEM((128, 3 * LANES), jnp.float32),
-            pltpu.VMEM((4, 128, LANES), jnp.float32),
+            pltpu.VMEM((16, 32), f32),
+            pltpu.VMEM((16, 32), f32),
+            pltpu.VMEM((ROWS, LANES), f32),
+            dma((6,)),
+            dma((3, 4)),
+            pltpu.VMEM((16, 96, LANES), f32),
+            pltpu.VMEM((16, 72, LANES), f32),
+            pltpu.VMEM((16, 96, LANES), f32),
+            pltpu.VMEM((8, 72, LANES), f32),
+            pltpu.VMEM((8, 96, LANES), f32),
+            pltpu.VMEM((8, 96, LANES), f32),
+            pltpu.VMEM((8, 96, LANES), f32),
+            pltpu.VMEM((16, 96, LANES), f32),
+            pltpu.VMEM((8, 1024), f32),
+            pltpu.VMEM((128, 3 * LANES), f32),
+            pltpu.VMEM((4, 128, LANES), f32),
+            dma(()),
+            dma((16,)),
+            dma(()),
             dma((16,)),
             dma((16,)),
             dma((16,)),
@@ -598,7 +640,7 @@
             dma((8,)),
         ],
         compiler_params=pltpu.CompilerParams(
-            collective_id=0, has_side_effects=True, vmem_limit_bytes=63 * 1024 * 1024
+            collective_id=0, has_side_effects=True, vmem_limit_bytes=VMEM_KERNEL
         ),
     )(
         disp.reshape(96, 1024),
@@ -609,8 +651,30 @@
         group_ids[None],
         diag_stiff.T,
         cross_stiff.T,
+        jnp.asarray(table),
+    )
+    out = jax.ShapeDtypeStruct((3, 32, 16, HALF), f32)
+    fields = pl.BlockSpec((16, 3, 8, LANES), lambda b: (0, 0, b, 0))
+    results = pl.BlockSpec((3, 8, 16, HALF), lambda b: (0, b, 0, 0))
+    residual, jvp = pl.pallas_call(
+        to_diameters,
+        grid=(4,),
+        out_shape=(out, out),
+        in_specs=[
+            fields,
+            fields,
+            pl.BlockSpec((1, 128, LANES), lambda b: (b, 0, 0)),
+            pl.BlockSpec((128, LANES), lambda b: (0, 0)),
+            results,
+        ],
+        out_specs=(results, results),
+        compiler_params=pltpu.CompilerParams(vmem_limit_bytes=VMEM_KERNEL),
+    )(
+        x_in.reshape(16, 3, 32, LANES),
+        l_in.reshape(16, 3, 32, LANES),
+        linear,
+        jnp.asarray(table[ROW_LOAD : ROW_LOAD + 128]),
         jnp.swapaxes(excitation, 2, 3),
-        table,
     )
     return (jnp.swapaxes(residual, 2, 3), jnp.swapaxes(jvp, 2, 3))
 

time: 46.4 us -> 46.8 us (level)
  Pallas kernels: 42.6 us -> 46 us
  local copies, waits for them, and re-layouts: 3.02 us -> 0 us
    pallas_call x1 -> x2, Pallas kernels: 42.6 us -> 46 us  [the longest x1 41.4 us: body_in_kernel(): pl.pallas_call(kernel, out_shape=(jax.ShapeDtypeStruct((16, 96, LANES), f...]
    unnamed x4 -> x0, local copies, waits for them, and re-layouts: 3.02 us -> none
where the time goes in v3:
time: 46.8 us; the launch traced here: 46.6 us
  Pallas kernels  46 us (98%)
  between operations  0.64 us (1%)
    pallas_call x1, Pallas kernels, body_in_kernel(): pl.pallas_call(kernel, out_shape=(jax.ShapeDtypeStruct((16, 96, LANES), f...  41.4 us
    pallas_call x1, Pallas kernels, body_in_kernel(): pl.pallas_call(to_diameters, grid=(4,), out_shape=(out, out), in_specs=[f...  4.51 us

profile of v3, /device:TPU:0, one launch (start us, length us, event | category | flops | bytes accessed | tf_op | source)
XLA Modules:
  0.0 46.6 jit_solution(4671696735552794932)
XLA Ops:
  0.6 41.4 %shard_map.122 = (f32[16,96,128]{2,1,0:T(8,128)}, f32[16,96,128]{2,1,0:T(8,128)}, f32[4,128,128]{2,1,0:T(8,128)}) custom-call(f32[96,1024]{1,0:T(8,128)} %bitcast.17, f32[96,1024]{1,0:T(8,128)} %bitcast.18, s32[128,1024]{1,0:T(8,128)} %bitcast.16, f32[4,1024]{1,0:T(4,128)} %bitcast.19, f32[1,16]{1,0:T(1,128)} %bitcast.22, s32[1,16]{1,0:T(1,128)} %bitcast.23, ...), custom_call_target="tpu_custom_call" | custom-call | tf_op jit(solution)/shard_map/pallas_call | solution.py:598
  42.1 4.5 %shard_map.123 = (f32[3,32,16,64]{3,2,1,0:T(8,128)}, f32[3,32,16,64]{3,2,1,0:T(8,128)}) custom-call(f32[16,3,32,128]{3,2,1,0:T(8,128)} %bitcast.14, f32[16,3,32,128]{3,2,1,0:T(8,128)} %bitcast.15, f32[4,128,128]{2,1,0:T(8,128)} %get-tuple-element.9.linear, f32[128,128]{1,0:T(8,128)} %constant.5.clone.reaction, f32[3,32,16,64]{3,2,1,0:T(8,128)} %bitcast.13), custom_call_target="tpu_custom_call" | custom-call | tf_op jit(solution)/shard_map/pallas_call | solution.py:659

commit v4 on v3

--- a/solution.py
+++ b/solution.py
@@ -185,11 +185,11 @@
     return jnp.dot(a, b, preferred_element_type=jnp.float32, precision=precision)
 
 
-SEND_ORDER = ((2, 0, 3, 1), (0, 1, 2, 3), (3, 2, 1, 0), (1, 3, 0, 2))
+SEND_ORDER = ((0, 2, 3, 1), (1, 0, 2, 3), (2, 3, 1, 0), (3, 1, 0, 2))
 PAIR_ORDER = (
     (0, 1, 2, 6, 7, 3, 4, 5),
-    (2, 6, 7, 0, 1, 3, 4, 5),
-    (4, 0, 5, 6, 7, 1, 2, 3),
+    (2, 6, 3, 4, 5, 7, 0, 1),
+    (4, 0, 1, 2, 3, 5, 6, 7),
     (6, 4, 5, 7, 0, 1, 2, 3),
 )
 
@@ -343,25 +343,28 @@
     mine_here = lax.rem(me, 2) == h
     core, x = lax.rem(me, 2), lax.rem(g0, 2)
 
-    def send(k, carry):
+    def prepare(k):
         z = at_step(send_order, k)
         for i in range(3):
             part(i, z).wait()
-
-        @pl.when(k == 0)
-        def _():
-            fetches[0].wait()
-            params8[0:4, :] = params[...]
-            params8[4:8, :] = params[...]
-
         pack(2 * z)
         pack(2 * z + 1)
 
+    def send(z, q):
+        to = 4 * z + 2 * lax.rem(q + core, 2) + lax.rem(q // 2 + x, 2)
+
+        @pl.when(to != me)
+        def _():
+            x_copy(to, me).start()
+
+            @pl.when(mine_here)
+            def _():
+                s_copy(to, me).start()
+
+    def first_sends(k, carry):
+        prepare(k)
+
         @pl.when(k == 0)
-        def _():
-            pl.semaphore_wait(barrier, sectors)
-
-        @pl.when(z == z0)
         def _():
             x_in[me] = x_out[me]
 
@@ -369,20 +372,18 @@
             def _():
                 s_in[g0] = s_out[me]
 
+            pl.semaphore_wait(barrier, sectors)
+
         for q in range(4):
-            to = 4 * z + 2 * lax.rem(q + core, 2) + lax.rem(q // 2 + x, 2)
-
-            @pl.when(to != me)
-            def _():
-                x_copy(to, me).start()
-
-                @pl.when(mine_here)
-                def _():
-                    s_copy(to, me).start()
-
+            send(at_step(send_order, k), q)
         return carry
 
-    lax.fori_loop(0, 4, send, 0)
+    fetches[0].wait()
+    params8[0:4, :] = params[...]
+    params8[4:8, :] = params[...]
+    lax.fori_loop(0, 2, first_sends, 0)
+    prepare(2)
+    prepare(3)
     for fetch in fetches[1:]:
         fetch.wait()
 
@@ -516,6 +517,12 @@
     hand_over(jnp.int32(0))
 
     def turn(j, carry):
+        @pl.when(j < 4)
+        def _():
+            z = at_step(send_order, 2 + j // 2)
+            for q in range(2):
+                send(z, 2 * lax.rem(j, 2) + q)
+
         @pl.when(j < pairs - 1)
         def _():
             hand_over(j + 1)

time: 46.8 us -> 48.5 us (1.036)
  Pallas kernels: 46 us -> 47.7 us
    pallas_call x1, Pallas kernels: 41.4 us -> 43.1 us  [body_in_kernel(): pl.pallas_call(kernel, out_shape=(jax.ShapeDtypeStruct((16, 96, LANES), f...]
where the time goes in v4:
time: 48.5 us; the launch traced here: 48.3 us
  Pallas kernels  47.7 us (98%)
  between operations  0.64 us (1%)
    pallas_call x1, Pallas kernels, body_in_kernel(): pl.pallas_call(kernel, out_shape=(jax.ShapeDtypeStruct((16, 96, LANES), f...  43.1 us
    pallas_call x1, Pallas kernels, body_in_kernel(): pl.pallas_call(to_diameters, grid=(4,), out_shape=(out, out), in_specs=[f...  4.51 us

profile of v4, /device:TPU:0, one launch (start us, length us, event | category | flops | bytes accessed | tf_op | source)
XLA Modules:
  0.0 48.3 jit_solution(9981712623060758182)
XLA Ops:
  0.6 43.1 %shard_map.122 = (f32[16,96,128]{2,1,0:T(8,128)}, f32[16,96,128]{2,1,0:T(8,128)}, f32[4,128,128]{2,1,0:T(8,128)}) custom-call(f32[96,1024]{1,0:T(8,128)} %bitcast.17, f32[96,1024]{1,0:T(8,128)} %bitcast.18, s32[128,1024]{1,0:T(8,128)} %bitcast.16, f32[4,1024]{1,0:T(4,128)} %bitcast.19, f32[1,16]{1,0:T(1,128)} %bitcast.22, s32[1,16]{1,0:T(1,128)} %bitcast.23, ...), custom_call_target="tpu_custom_call" | custom-call | tf_op jit(solution)/shard_map/pallas_call | solution.py:605
  43.8 4.5 %shard_map.123 = (f32[3,32,16,64]{3,2,1,0:T(8,128)}, f32[3,32,16,64]{3,2,1,0:T(8,128)}) custom-call(f32[16,3,32,128]{3,2,1,0:T(8,128)} %bitcast.14, f32[16,3,32,128]{3,2,1,0:T(8,128)} %bitcast.15, f32[4,128,128]{2,1,0:T(8,128)} %get-tuple-element.9.linear, f32[128,128]{1,0:T(8,128)} %constant.5.clone.reaction, f32[3,32,16,64]{3,2,1,0:T(8,128)} %bitcast.13), custom_call_target="tpu_custom_call" | custom-call | tf_op jit(solution)/shard_map/pallas_call | solution.py:666

commit v5 on v3

--- a/solution.py
+++ b/solution.py
@@ -188,8 +188,8 @@
 SEND_ORDER = ((2, 0, 3, 1), (0, 1, 2, 3), (3, 2, 1, 0), (1, 3, 0, 2))
 PAIR_ORDER = (
     (0, 1, 2, 6, 7, 3, 4, 5),
-    (2, 6, 7, 0, 1, 3, 4, 5),
-    (4, 0, 5, 6, 7, 1, 2, 3),
+    (2, 6, 3, 4, 5, 7, 0, 1),
+    (4, 0, 1, 2, 3, 5, 6, 7),
     (6, 4, 5, 7, 0, 1, 2, 3),
 )
 
@@ -209,9 +209,8 @@
     diag_hbm,
     cross_hbm,
     table_hbm,
-    x_hbm,
-    l_hbm,
-    linear_hbm,
+    residual,
+    jvp,
     disp,
     direction,
     states,
@@ -234,9 +233,6 @@
     params8,
     tractions,
     linear,
-    x_kept,
-    l_kept,
-    linear_kept,
     x_sent,
     x_got,
     s_sent,
@@ -253,6 +249,7 @@
     g0 = me // 2
     z0 = me // 4
     partner = (me, 1 - h)
+    side = lax.rem(h + lax.rem(g0, 2), 2)
 
     def by_z(values):
         out = jnp.int32(values[3])
@@ -340,8 +337,11 @@
             device_id_type=MESH,
         )
 
-    mine_here = lax.rem(me, 2) == h
     core, x = lax.rem(me, 2), lax.rem(g0, 2)
+    mine_here = core == side
+
+    def states_for(to):
+        return core == lax.rem(h + lax.rem(to // 2, 2), 2)
 
     def send(k, carry):
         z = at_step(send_order, k)
@@ -376,7 +376,7 @@
             def _():
                 x_copy(to, me).start()
 
-                @pl.when(mine_here)
+                @pl.when(states_for(to))
                 def _():
                     s_copy(to, me).start()
 
@@ -412,13 +412,6 @@
         c = jnp.sum(jnp.where(chosen, cross_rows, 0.0), axis=1, keepdims=True)
         linear[b] = same * (d * plain + c * turned_back + tuned)
 
-    linear_copy = pltpu.make_async_copy(linear, linear_hbm, linear_kept)
-    linear_copy.start()
-    x_keep = pltpu.make_async_copy(x_in, x_hbm, x_kept)
-
-    def l_keep(sector):
-        return pltpu.make_async_copy(l_in.at[sector], l_hbm.at[sector], l_kept.at[sector])
-
     def r_copy(j):
         return pltpu.make_async_remote_copy(
             src_ref=r_out.at[j],
@@ -459,13 +452,13 @@
         def _():
             arrive(lax.rem(2 * g + 2, sectors))
 
-        other = 2 * g + 1 - h
+        other = 2 * g + 1 - side
         r_out[j] = x_in[other] - x_in[lax.rem(other + 1, sectors)]
         r_copy(j).start()
 
     def contact(j):
         g = pair(j)
-        sector = 2 * g + h
+        sector = 2 * g + side
         own = x_in[sector] - x_in[lax.rem(sector + 1, sectors)]
 
         @pl.when(sector != me)
@@ -511,7 +504,6 @@
         l_copy(j, sector).start()
         for i in range(3):
             l_in[sector, 32 * i : 32 * i + 32, :] = loads[0:32, LANES * i : LANES * (i + 1)]
-        l_keep(sector).start()
 
     hand_over(jnp.int32(0))
 
@@ -520,28 +512,35 @@
         def _():
             hand_over(j + 1)
 
-        @pl.when(j == pairs - 2)
-        def _():
-            x_keep.start()
-
         contact(j)
         return carry
 
     lax.fori_loop(0, pairs, turn, 0)
 
     def loads_here(j, carry):
-        sector = 2 * pair(j) + 1 - h
-        l_copy(j, sector).wait_recv()
-        l_keep(sector).start()
+        l_copy(j, 2 * pair(j) + 1 - side).wait_recv()
         return carry
 
     lax.fori_loop(0, pairs, loads_here, 0)
+    reaction = table[ROW_LOAD : ROW_LOAD + 128, :]
+    for b in range(4):
+        matrix = jnp.concatenate([linear[b], reaction], 1)
+        columns = []
+        for i in range(3):
+            at = slice(32 * i + 8 * b, 32 * i + 8 * b + 8)
+            field = [x_in[:, at, :].reshape(128, LANES), l_in[:, at, :].reshape(128, LANES)]
+            columns.append(jnp.concatenate(field, 0))
+        out = product(matrix, jnp.concatenate(columns, 1))
+        for i in range(3):
+            both = out[:, LANES * i : LANES * (i + 1)]
+            residual[i, 8 * b : 8 * b + 8] = both.reshape(8, 16, LANES)
+            jvp[i, 8 * b : 8 * b + 8] = pltpu.roll(both, HALF, 1).reshape(8, 16, LANES)
 
     def sent(i, carry):
         to = lax.rem(me + i, sectors)
         x_copy(to, me).wait_send()
 
-        @pl.when(mine_here)
+        @pl.when(states_for(to))
         def _():
             s_copy(to, me).wait_send()
 
@@ -551,33 +550,10 @@
 
     def sent_back(j, carry):
         r_copy(j).wait_send()
-        l_copy(j, 2 * pair(j) + h).wait_send()
+        l_copy(j, 2 * pair(j) + side).wait_send()
         return carry
 
     lax.fori_loop(0, pairs, sent_back, 0)
-    linear_copy.wait()
-    x_keep.wait()
-
-    def kept(i, carry):
-        l_keep(i).wait()
-        return carry
-
-    lax.fori_loop(0, sectors, kept, 0)
-
-
-def to_diameters(x_in, l_in, linear, reaction, excitation, residual, jvp):
-    matrix = jnp.concatenate([linear[0], reaction[...]], 1)
-    columns = []
-    for i in range(3):
-        field = [x_in[:, i].reshape(128, LANES), l_in[:, i].reshape(128, LANES)]
-        columns.append(jnp.concatenate(field, 0))
-    out = product(matrix, jnp.concatenate(columns, 1), lax.Precision.HIGH)
-    for i in range(3):
-        both = out[:, LANES * i : LANES * (i + 1)]
-        first = both[:, 0:HALF].reshape(8, 16, HALF)
-        second = pltpu.roll(both, HALF, 1)[:, 0:HALF].reshape(8, 16, HALF)
-        residual[i] = first - excitation[i]
-        jvp[i] = second
 
 
 def body_in_kernel(
@@ -595,15 +571,13 @@
     dma = pltpu.SemaphoreType.DMA
     f32 = jnp.float32
     table = constant_table(16, 64, 128)
-    x_in, l_in, linear = pl.pallas_call(
+    vmem = pl.BlockSpec(memory_space=pltpu.VMEM)
+    out = jax.ShapeDtypeStruct((3, 32, 16, LANES), f32)
+    residual, jvp = pl.pallas_call(
         kernel,
-        out_shape=(
-            jax.ShapeDtypeStruct((16, 96, LANES), f32),
-            jax.ShapeDtypeStruct((16, 96, LANES), f32),
-            jax.ShapeDtypeStruct((4, 128, LANES), f32),
-        ),
+        out_shape=(out, out),
         in_specs=[hbm] * 9,
-        out_specs=(hbm, hbm, hbm),
+        out_specs=(vmem, vmem),
         scratch_shapes=[
             pltpu.VMEM((96, 1024), f32),
             pltpu.VMEM((96, 1024), f32),
@@ -627,9 +601,6 @@
             pltpu.VMEM((8, 1024), f32),
             pltpu.VMEM((128, 3 * LANES), f32),
             pltpu.VMEM((4, 128, LANES), f32),
-            dma(()),
-            dma((16,)),
-            dma(()),
             dma((16,)),
             dma((16,)),
             dma((16,)),
@@ -653,30 +624,8 @@
         cross_stiff.T,
         jnp.asarray(table),
     )
-    out = jax.ShapeDtypeStruct((3, 32, 16, HALF), f32)
-    fields = pl.BlockSpec((16, 3, 8, LANES), lambda b: (0, 0, b, 0))
-    results = pl.BlockSpec((3, 8, 16, HALF), lambda b: (0, b, 0, 0))
-    residual, jvp = pl.pallas_call(
-        to_diameters,
-        grid=(4,),
-        out_shape=(out, out),
-        in_specs=[
-            fields,
-            fields,
-            pl.BlockSpec((1, 128, LANES), lambda b: (b, 0, 0)),
-            pl.BlockSpec((128, LANES), lambda b: (0, 0)),
-            results,
-        ],
-        out_specs=(results, results),
-        compiler_params=pltpu.CompilerParams(vmem_limit_bytes=VMEM_KERNEL),
-    )(
-        x_in.reshape(16, 3, 32, LANES),
-        l_in.reshape(16, 3, 32, LANES),
-        linear,
-        jnp.asarray(table[ROW_LOAD : ROW_LOAD + 128]),
-        jnp.swapaxes(excitation, 2, 3),
-    )
-    return (jnp.swapaxes(residual, 2, 3), jnp.swapaxes(jvp, 2, 3))
+    residual = residual[..., :HALF] - jnp.swapaxes(excitation, 2, 3)
+    return (jnp.swapaxes(residual, 2, 3), jnp.swapaxes(jvp[..., :HALF], 2, 3))
 
 
 def solution(mesh):

time: 46.8 us -> 46.9 us (level)
  the two profiles are of different devices: /device:TPU:0 before, /device:TPU:19 now
where the time goes in v5:
time: 46.9 us; the launch traced here: 46.8 us
  Pallas kernels  43.4 us (93%)
  other arithmetic  2.69 us (6%)
  between operations  0.66 us (1%)
    pallas_call x1, Pallas kernels, body_in_kernel(): pl.pallas_call(kernel, out_shape=(out, out), in_specs=[hbm] * 9, out_spec...  43.4 us
    transpose x1, other arithmetic, body_in_kernel(): return (jnp.swapaxes(residual, 2, 3), jnp.swapaxes(jvp[..., :HALF], 2, 3))  2.69 us

profile of v5, /device:TPU:19, one launch (start us, length us, event | category | flops | bytes accessed | tf_op | source)
XLA Modules:
  0.0 46.8 jit_solution(15461440790361445827)
XLA Ops:
  0.6 0.0 copy-start
  0.6 43.4 %shard_map.113 = (f32[3,32,16,128]{3,2,1,0:T(8,128)}, f32[3,32,16,128]{3,2,1,0:T(8,128)}) custom-call(f32[96,1024]{1,0:T(8,128)} %bitcast.17, f32[96,1024]{1,0:T(8,128)} %bitcast.18, s32[128,1024]{1,0:T(8,128)} %bitcast.16, f32[4,1024]{1,0:T(4,128)} %bitcast.19, f32[1,16]{1,0:T(1,128)} %bitcast.22, s32[1,16]{1,0:T(1,128)} %bitcast.23, f32[16,32]{1,0:T(8,128)} %bitcast.20, ...), custom_call_target="tpu_custom_call" | custom-call | tf_op jit(solution)/shard_map/pallas_call | solution.py:576
  44.1 0.0 copy-done
  44.1 2.7 %fusion = (f32[3,32,64,16]{2,3,1,0:T(8,128)}, f32[3,32,64,16]{2,3,1,0:T(8,128)}) fusion(f32[3,32,64,16]{2,3,1,0:T(8,128)S(1)} %copy-done, f32[3,32,16,128]{3,2,1,0:T(8,128)} %get-tuple-element.4, f32[3,32,16,128]{3,2,1,0:T(8,128)} %get-tuple-element.5), kind=kLoop, calls=%fused_computation.1 | loop fusion | flops 98304 | bytes 1966080 | tf_op jit(solution)/shard_map/transpose | solution.py:628
Async XLA Ops:
  0.6 43.4 %copy-start = (f32[3,32,64,16]{2,3,1,0:T(8,128)S(1)}, f32[3,32,64,16]{2,3,1,0:T(8,128)}, u32[]{:S(2)}) copy-start(f32[3,32,64,16]{2,3,1,0:T(8,128)} %param.18) | copy-start | bytes 1179652

commit v6 on v5

--- a/solution.py
+++ b/solution.py
@@ -189,9 +189,12 @@
 PAIR_ORDER = (
     (0, 1, 2, 6, 7, 3, 4, 5),
     (2, 6, 3, 4, 5, 7, 0, 1),
-    (4, 0, 1, 2, 3, 5, 6, 7),
+    (4, 0, 5, 6, 7, 1, 2, 3),
     (6, 4, 5, 7, 0, 1, 2, 3),
 )
+
+
+LATE = ((0, 2, 4), (0, 1, 4), (0, 1, 4), (0, 2, 4))
 
 
 def seen(z, k, step):
@@ -233,6 +236,7 @@
     params8,
     tractions,
     linear,
+    moved_on,
     x_sent,
     x_got,
     s_sent,
@@ -265,6 +269,7 @@
 
     send_order = [by_z([SEND_ORDER[z][k] for z in range(4)]) for k in range(4)]
     pair_order = [by_z([PAIR_ORDER[z][k] for z in range(4)]) for k in range(8)]
+    late = [by_z([int(k in LATE[z]) for z in range(4)]) for k in range(8)]
     new_first = [by_z([seen(z, k, -1) for z in range(4)]) for k in range(8)]
     new_last = [by_z([seen(z, k, 1) for z in range(4)]) for k in range(8)]
 
@@ -369,16 +374,18 @@
             def _():
                 s_in[g0] = s_out[me]
 
-        for q in range(4):
-            to = 4 * z + 2 * lax.rem(q + core, 2) + lax.rem(q // 2 + x, 2)
+        tos = [4 * z + 2 * lax.rem(q + core, 2) + lax.rem(q // 2 + x, 2) for q in range(4)]
+        for to in tos:
 
             @pl.when(to != me)
-            def _():
+            def _(to=to):
                 x_copy(to, me).start()
 
-                @pl.when(states_for(to))
-                def _():
-                    s_copy(to, me).start()
+        for to in tos:
+
+            @pl.when(jnp.logical_and(to != me, states_for(to)))
+            def _(to=to):
+                s_copy(to, me).start()
 
         return carry
 
@@ -508,14 +515,28 @@
     hand_over(jnp.int32(0))
 
     def turn(j, carry):
-        @pl.when(j < pairs - 1)
+        waits = at_step(late, j)
+
+        @pl.when(jnp.logical_and(j < pairs - 1, waits == 0))
         def _():
             hand_over(j + 1)
 
         contact(j)
+
+        @pl.when(jnp.logical_and(j < pairs - 1, waits == 1))
+        def _():
+            hand_over(j + 1)
+
         return carry
 
     lax.fori_loop(0, pairs, turn, 0)
+
+    def columns(fields, b):
+        rows = [slice(32 * i + 8 * b, 32 * i + 8 * b + 8) for i in range(3)]
+        return jnp.concatenate([fields[:, at, :].reshape(128, LANES) for at in rows], 1)
+
+    for b in range(4):
+        moved_on[b] = product(linear[b], columns(x_in, b))
 
     def loads_here(j, carry):
         l_copy(j, 2 * pair(j) + 1 - side).wait_recv()
@@ -524,13 +545,7 @@
     lax.fori_loop(0, pairs, loads_here, 0)
     reaction = table[ROW_LOAD : ROW_LOAD + 128, :]
     for b in range(4):
-        matrix = jnp.concatenate([linear[b], reaction], 1)
-        columns = []
-        for i in range(3):
-            at = slice(32 * i + 8 * b, 32 * i + 8 * b + 8)
-            field = [x_in[:, at, :].reshape(128, LANES), l_in[:, at, :].reshape(128, LANES)]
-            columns.append(jnp.concatenate(field, 0))
-        out = product(matrix, jnp.concatenate(columns, 1))
+        out = moved_on[b] + product(reaction, columns(l_in, b))
         for i in range(3):
             both = out[:, LANES * i : LANES * (i + 1)]
             residual[i, 8 * b : 8 * b + 8] = both.reshape(8, 16, LANES)
@@ -601,6 +616,7 @@
             pltpu.VMEM((8, 1024), f32),
             pltpu.VMEM((128, 3 * LANES), f32),
             pltpu.VMEM((4, 128, LANES), f32),
+            pltpu.VMEM((4, 128, 3 * LANES), f32),
             dma((16,)),
             dma((16,)),
             dma((16,)),

time: 46.9 us -> 47.3 us (level)
  the two profiles are of different devices: /device:TPU:19 before, /device:TPU:8 now
where the time goes in v6:
time: 47.3 us; the launch traced here: 47.2 us
  Pallas kernels  43.8 us (93%)
  other arithmetic  2.69 us (6%)
  between operations  0.66 us (1%)
    pallas_call x1, Pallas kernels, body_in_kernel(): pl.pallas_call(kernel, out_shape=(out, out), in_specs=[hbm] * 9, out_spec...  43.8 us
    transpose x1, other arithmetic, body_in_kernel(): return (jnp.swapaxes(residual, 2, 3), jnp.swapaxes(jvp[..., :HALF], 2, 3))  2.69 us

profile of v6, /device:TPU:8, one launch (start us, length us, event | category | flops | bytes accessed | tf_op | source)
XLA Modules:
  0.0 47.2 jit_solution(17186415193474933515)
XLA Ops:
  0.6 0.0 copy-start
  0.6 43.8 %shard_map.113 = (f32[3,32,16,128]{3,2,1,0:T(8,128)}, f32[3,32,16,128]{3,2,1,0:T(8,128)}) custom-call(f32[96,1024]{1,0:T(8,128)} %bitcast.17, f32[96,1024]{1,0:T(8,128)} %bitcast.18, s32[128,1024]{1,0:T(8,128)} %bitcast.16, f32[4,1024]{1,0:T(4,128)} %bitcast.19, f32[1,16]{1,0:T(1,128)} %bitcast.22, s32[1,16]{1,0:T(1,128)} %bitcast.23, f32[16,32]{1,0:T(8,128)} %bitcast.20, ...), custom_call_target="tpu_custom_call" | custom-call | tf_op jit(solution)/shard_map/pallas_call | solution.py:591
  44.5 0.0 copy-done
  44.5 2.7 %fusion = (f32[3,32,64,16]{2,3,1,0:T(8,128)}, f32[3,32,64,16]{2,3,1,0:T(8,128)}) fusion(f32[3,32,64,16]{2,3,1,0:T(8,128)S(1)} %copy-done, f32[3,32,16,128]{3,2,1,0:T(8,128)} %get-tuple-element.4, f32[3,32,16,128]{3,2,1,0:T(8,128)} %get-tuple-element.5), kind=kLoop, calls=%fused_computation.1 | loop fusion | flops 98304 | bytes 1966080 | tf_op jit(solution)/shard_map/transpose | solution.py:644
Async XLA Ops:
  0.6 43.8 %copy-start = (f32[3,32,64,16]{2,3,1,0:T(8,128)S(1)}, f32[3,32,64,16]{2,3,1,0:T(8,128)}, u32[]{:S(2)}) copy-start(f32[3,32,64,16]{2,3,1,0:T(8,128)} %param.18) | copy-start | bytes 1179652

commit v7 on v6

--- a/solution.py
+++ b/solution.py
@@ -188,13 +188,10 @@
 SEND_ORDER = ((2, 0, 3, 1), (0, 1, 2, 3), (3, 2, 1, 0), (1, 3, 0, 2))
 PAIR_ORDER = (
     (0, 1, 2, 6, 7, 3, 4, 5),
-    (2, 6, 3, 4, 5, 7, 0, 1),
+    (2, 6, 7, 0, 1, 3, 4, 5),
     (4, 0, 5, 6, 7, 1, 2, 3),
     (6, 4, 5, 7, 0, 1, 2, 3),
 )
-
-
-LATE = ((0, 2, 4), (0, 1, 4), (0, 1, 4), (0, 2, 4))
 
 
 def seen(z, k, step):
@@ -253,7 +250,7 @@
     g0 = me // 2
     z0 = me // 4
     partner = (me, 1 - h)
-    side = lax.rem(h + lax.rem(g0, 2), 2)
+    side = h
 
     def by_z(values):
         out = jnp.int32(values[3])
@@ -269,7 +266,6 @@
 
     send_order = [by_z([SEND_ORDER[z][k] for z in range(4)]) for k in range(4)]
     pair_order = [by_z([PAIR_ORDER[z][k] for z in range(4)]) for k in range(8)]
-    late = [by_z([int(k in LATE[z]) for z in range(4)]) for k in range(8)]
     new_first = [by_z([seen(z, k, -1) for z in range(4)]) for k in range(8)]
     new_last = [by_z([seen(z, k, 1) for z in range(4)]) for k in range(8)]
 
@@ -345,9 +341,6 @@
     core, x = lax.rem(me, 2), lax.rem(g0, 2)
     mine_here = core == side
 
-    def states_for(to):
-        return core == lax.rem(h + lax.rem(to // 2, 2), 2)
-
     def send(k, carry):
         z = at_step(send_order, k)
         for i in range(3):
@@ -381,11 +374,9 @@
             def _(to=to):
                 x_copy(to, me).start()
 
-        for to in tos:
-
-            @pl.when(jnp.logical_and(to != me, states_for(to)))
-            def _(to=to):
-                s_copy(to, me).start()
+                @pl.when(mine_here)
+                def _():
+                    s_copy(to, me).start()
 
         return carry
 
@@ -515,18 +506,11 @@
     hand_over(jnp.int32(0))
 
     def turn(j, carry):
-        waits = at_step(late, j)
-
-        @pl.when(jnp.logical_and(j < pairs - 1, waits == 0))
+        @pl.when(j < pairs - 1)
         def _():
             hand_over(j + 1)
 
         contact(j)
-
-        @pl.when(jnp.logical_and(j < pairs - 1, waits == 1))
-        def _():
-            hand_over(j + 1)
-
         return carry
 
     lax.fori_loop(0, pairs, turn, 0)
@@ -555,7 +539,7 @@
         to = lax.rem(me + i, sectors)
         x_copy(to, me).wait_send()
 
-        @pl.when(states_for(to))
+        @pl.when(mine_here)
         def _():
             s_copy(to, me).wait_send()
 

time: 47.3 us -> 46.1 us (0.975)
  the two profiles are of different devices: /device:TPU:8 before, /device:TPU:0 now
where the time goes in v7:
time: 46.1 us; the launch traced here: 46 us
  Pallas kernels  42.6 us (92%)
  other arithmetic  2.69 us (6%)
  between operations  0.66 us (1%)
    pallas_call x1, Pallas kernels, body_in_kernel(): pl.pallas_call(kernel, out_shape=(out, out), in_specs=[hbm] * 9, out_spec...  42.6 us
    transpose x1, other arithmetic, body_in_kernel(): return (jnp.swapaxes(residual, 2, 3), jnp.swapaxes(jvp[..., :HALF], 2, 3))  2.69 us

profile of v7, /device:TPU:0, one launch (start us, length us, event | category | flops | bytes accessed | tf_op | source)
XLA Modules:
  0.0 46.0 jit_solution(5083269549652138042)
XLA Ops:
  0.6 0.0 copy-start
  0.6 42.6 %shard_map.113 = (f32[3,32,16,128]{3,2,1,0:T(8,128)}, f32[3,32,16,128]{3,2,1,0:T(8,128)}) custom-call(f32[96,1024]{1,0:T(8,128)} %bitcast.17, f32[96,1024]{1,0:T(8,128)} %bitcast.18, s32[128,1024]{1,0:T(8,128)} %bitcast.16, f32[4,1024]{1,0:T(4,128)} %bitcast.19, f32[1,16]{1,0:T(1,128)} %bitcast.22, s32[1,16]{1,0:T(1,128)} %bitcast.23, f32[16,32]{1,0:T(8,128)} %bitcast.20, ...), custom_call_target="tpu_custom_call" | custom-call | tf_op jit(solution)/shard_map/pallas_call | solution.py:575
  43.3 0.0 copy-done
  43.3 2.7 %fusion = (f32[3,32,64,16]{2,3,1,0:T(8,128)}, f32[3,32,64,16]{2,3,1,0:T(8,128)}) fusion(f32[3,32,64,16]{2,3,1,0:T(8,128)S(1)} %copy-done, f32[3,32,16,128]{3,2,1,0:T(8,128)} %get-tuple-element.4, f32[3,32,16,128]{3,2,1,0:T(8,128)} %get-tuple-element.5), kind=kLoop, calls=%fused_computation.1 | loop fusion | flops 98304 | bytes 1966080 | tf_op jit(solution)/shard_map/transpose | solution.py:628
Async XLA Ops:
  0.6 42.6 %copy-start = (f32[3,32,64,16]{2,3,1,0:T(8,128)S(1)}, f32[3,32,64,16]{2,3,1,0:T(8,128)}, u32[]{:S(2)}) copy-start(f32[3,32,64,16]{2,3,1,0:T(8,128)} %param.18) | copy-start | bytes 1179652

commit v8 on v7

--- a/solution.py
+++ b/solution.py
@@ -185,7 +185,7 @@
     return jnp.dot(a, b, preferred_element_type=jnp.float32, precision=precision)
 
 
-SEND_ORDER = ((2, 0, 3, 1), (0, 1, 2, 3), (3, 2, 1, 0), (1, 3, 0, 2))
+SEND_ORDER = ((0, 2, 3, 1), (1, 0, 2, 3), (2, 3, 1, 0), (3, 1, 0, 2))
 PAIR_ORDER = (
     (0, 1, 2, 6, 7, 3, 4, 5),
     (2, 6, 7, 0, 1, 3, 4, 5),

time: 46.1 us -> 46.4 us (level)
  no operation moved by 1% of the time
where the time goes in v8:
time: 46.4 us; the launch traced here: 46.2 us
  Pallas kernels  42.8 us (92%)
  other arithmetic  2.69 us (6%)
  between operations  0.66 us (1%)
    pallas_call x1, Pallas kernels, body_in_kernel(): pl.pallas_call(kernel, out_shape=(out, out), in_specs=[hbm] * 9, out_spec...  42.8 us
    transpose x1, other arithmetic, body_in_kernel(): return (jnp.swapaxes(residual, 2, 3), jnp.swapaxes(jvp[..., :HALF], 2, 3))  2.69 us

profile of v8, /device:TPU:0, one launch (start us, length us, event | category | flops | bytes accessed | tf_op | source)
XLA Modules:
  0.0 46.2 jit_solution(14454019883773804465)
XLA Ops:
  0.6 0.0 copy-start
  0.6 42.8 %shard_map.113 = (f32[3,32,16,128]{3,2,1,0:T(8,128)}, f32[3,32,16,128]{3,2,1,0:T(8,128)}) custom-call(f32[96,1024]{1,0:T(8,128)} %bitcast.17, f32[96,1024]{1,0:T(8,128)} %bitcast.18, s32[128,1024]{1,0:T(8,128)} %bitcast.16, f32[4,1024]{1,0:T(4,128)} %bitcast.19, f32[1,16]{1,0:T(1,128)} %bitcast.22, s32[1,16]{1,0:T(1,128)} %bitcast.23, f32[16,32]{1,0:T(8,128)} %bitcast.20, ...), custom_call_target="tpu_custom_call" | custom-call | tf_op jit(solution)/shard_map/pallas_call | solution.py:575
  43.5 0.0 copy-done
  43.5 2.7 %fusion = (f32[3,32,64,16]{2,3,1,0:T(8,128)}, f32[3,32,64,16]{2,3,1,0:T(8,128)}) fusion(f32[3,32,64,16]{2,3,1,0:T(8,128)S(1)} %copy-done, f32[3,32,16,128]{3,2,1,0:T(8,128)} %get-tuple-element.4, f32[3,32,16,128]{3,2,1,0:T(8,128)} %get-tuple-element.5), kind=kLoop, calls=%fused_computation.1 | loop fusion | flops 98304 | bytes 1966080 | tf_op jit(solution)/shard_map/transpose | solution.py:628
Async XLA Ops:
  0.6 42.9 %copy-start = (f32[3,32,64,16]{2,3,1,0:T(8,128)S(1)}, f32[3,32,64,16]{2,3,1,0:T(8,128)}, u32[]{:S(2)}) copy-start(f32[3,32,64,16]{2,3,1,0:T(8,128)} %param.18) | copy-start | bytes 1179652
